TPU v7x, 256 devices: a whole 4x4x8 slice. The times are simulated.
256 devices in a mesh: gx: 16 (over x, y), gy: 16 (over z, core).
Axes of the slice: x: 4, y: 4, z: 8, core: 2. Of those that a mesh axis runs over, the one named last changes fastest.
Arguments:
- populations: float32 [19, 128, 512, 128], P(None, 'gx', 'gy'), as said below
- fluid: int32 [128, 512, 128], P('gx', 'gy'), may hold values from 0 to 1
Outputs:
- velocity_image: float32 [3, 32, 128, 32], P(None, 'gx', None, 'gy')
- magnitude: float32 [32, 128, 32], P('gx', None, 'gy')
Inputs may be any that keep to these rules, and one draw needn't show every extreme that they name: `populations`: every population is positive.
All inputs are finite; a program needn't handle non-finite values.
Results may differ from a plain program's by a relative error of at most 0.00025.
Values sent between devices are 32-bit elements; how exact they have to be, the bound alone decides.
A program may use at most 128 MiB of HBM per device.

v0:
```python
import jax
import jax.numpy as jnp
from jax import lax
from jax.sharding import PartitionSpec as P

STEPS = 2


VELOCITIES = (
    (0, 0, 0),
    (1, 0, 0),
    (-1, 0, 0),
    (0, 1, 0),
    (0, -1, 0),
    (0, 0, 1),
    (0, 0, -1),
    (1, 1, 0),
    (-1, -1, 0),
    (1, -1, 0),
    (-1, 1, 0),
    (1, 0, 1),
    (-1, 0, -1),
    (1, 0, -1),
    (-1, 0, 1),
    (0, 1, 1),
    (0, -1, -1),
    (0, 1, -1),
    (0, -1, 1),
)
WEIGHTS = (1.0 / 3.0,) + (1.0 / 18.0,) * 6 + (1.0 / 36.0,) * 12
OPPOSITE = (0, 2, 1, 4, 3, 6, 5, 8, 7, 10, 9, 12, 11, 14, 13, 16, 15, 18, 17)
relax_rate = 1.0 / 0.6
velocity_scale = 0.002
spread_side = 0.25
spread_middle = 0.5


def extended_2(block, sides, width):
    for axis, dim in sides:
        count = lax.axis_size(axis)
        forward = [(i, i + 1) for i in range(count - 1)]
        backward = [(target, source) for source, target in forward]
        low = lax.ppermute(
            lax.slice_in_dim(block, block.shape[dim] - width, None, axis=dim), axis, forward
        )
        high = lax.ppermute(lax.slice_in_dim(block, 0, width, axis=dim), axis, backward)
        block = jnp.concatenate([low, block, high], axis=dim)
    return block


def moments(current):
    density = jnp.sum(current, axis=0)
    speeds = []
    for component in range(3):
        total = jnp.zeros_like(density)
        for channel in range(19):
            factor = VELOCITIES[channel][component]
            if factor == 1:
                total = total + current[channel]
            elif factor == -1:
                total = total - current[channel]
        speeds.append(total / density)
    return (density, speeds[0], speeds[1], speeds[2])


def collide(current):
    density, speed_x, speed_y, speed_z = moments(current)
    square = speed_x * speed_x + speed_y * speed_y + speed_z * speed_z
    relaxed = []
    for channel in range(19):
        along_x, along_y, along_z = VELOCITIES[channel]
        projected = along_x * speed_x + along_y * speed_y + along_z * speed_z
        balance = (
            WEIGHTS[channel]
            * density
            * (1.0 + 3.0 * projected + 4.5 * projected * projected - 1.5 * square)
        )
        relaxed.append(current[channel] - relax_rate * (current[channel] - balance))
    return jnp.stack(relaxed)


def propagate(padded, walls, relaxed):
    size_x, size_y, size_z = (relaxed.shape[1], relaxed.shape[2], relaxed.shape[3])
    moved = []
    for channel in range(19):
        along_x, along_y, along_z = VELOCITIES[channel]
        start_x, start_y, start_z = (1 - along_x, 1 - along_y, 1 - along_z)
        source = padded[
            channel,
            start_x : start_x + size_x,
            start_y : start_y + size_y,
            start_z : start_z + size_z,
        ]
        open_site = walls[
            start_x : start_x + size_x, start_y : start_y + size_y, start_z : start_z + size_z
        ]
        moved.append(jnp.where(open_site > 0, source, relaxed[OPPOSITE[channel]]))
    return jnp.stack(moved)


def voxel_sums(current, fluid):
    density, speed_x, speed_y, speed_z = moments(current)
    fluid_float = fluid.astype(jnp.float32)
    stacked = jnp.stack(
        [fluid_float * speed_x, fluid_float * speed_y, fluid_float * speed_z, fluid_float]
    )
    size_x, size_y, size_z = fluid.shape
    return stacked.reshape(4, size_x // 4, 4, size_y // 4, 4, size_z // 4, 4).sum(axis=(2, 4, 6))


def trim(extended, dimension):
    length = extended.shape[dimension] - 2
    return (
        spread_side * lax.slice_in_dim(extended, 0, length, axis=dimension)
        + spread_middle * lax.slice_in_dim(extended, 1, length + 1, axis=dimension)
        + spread_side * lax.slice_in_dim(extended, 2, length + 2, axis=dimension)
    )


def spread_axis(values, dimension):
    widths = [(1, 1) if other == dimension else (0, 0) for other in range(values.ndim)]
    return trim(jnp.pad(values, widths), dimension)


def spread_after(moved):
    extended = extended_2(moved, (("gx", 1), ("gy", 3)), 1)
    return spread_axis(trim(trim(extended, 1), 3), 2)


def local(populations, fluid):
    walls = extended_2(fluid, (("gx", 0), ("gy", 1)), 1)
    walls = jnp.pad(walls, ((0, 0), (0, 0), (1, 1)))
    current = populations
    for sweep_index in range(STEPS):
        relaxed = collide(current)
        extended = extended_2(relaxed, (("gx", 1), ("gy", 2)), 1)
        padded = jnp.pad(extended, ((0, 0), (0, 0), (0, 0), (1, 1)))
        current = propagate(padded, walls, relaxed)
    sums = voxel_sums(current, fluid)
    moved = lax.all_to_all(sums, "gy", split_axis=3, concat_axis=2, tiled=True)
    moved = spread_after(moved)
    velocity_image = moved[:3] / jnp.maximum(moved[3], 1.0) / velocity_scale
    magnitude = moved[3] / 64.0
    return (velocity_image, magnitude)


def solution(mesh):
    placed = (P(None, "gx", "gy", None), P("gx", "gy", None))
    return jax.shard_map(
        local,
        mesh=mesh,
        in_specs=placed,
        out_specs=(P(None, "gx", None, "gy"), P("gx", None, "gy")),
        check_vma=False,
    )
```

profile of v0, /device:TPU:7, one launch (start us, length us, event | category | flops | bytes accessed | tf_op | source)
XLA Modules:
  0.0 160.0 jit_solution(1207734053631379022)
XLA Ops:
  0.7 0.9 fusion.528
  1.5 3.2 %collective-permute-start = (s32[1,32,128]{2,1,0:T(8,128)S(1)}, s32[1,32,128]{2,1,0:T(8,128)S(1)}, u32[]{:S(2)}, u32[]{:S(2)}) collective-permute-start(s32[1,32,128]{2,1,0:T(8,128)S(1)} %get-tuple-element.121), channel_id=1, source_target_pairs={{0,16},{16,32},{32,48},{48,64},{64,80},{80,96},{96,112},{112,128},... | collective-permute-start | bytes 49160 | tf_op jit(solution)/shard_map/ppermute | solution.py:43
  4.7 1.9 %reduce_sum.136 = f32[8,32,128]{2,1,0:T(8,128)S(1)} reduce(f32[19,8,32,128]{3,2,1,0:T(8,128)} %param.2, f32[]{:T(128)} %constant.16.clone.1), dimensions={0}, to_apply=%region_0.1 | reduce | flops 589824 | bytes 2621444 | tf_op jit(solution)/shard_map/reduce_sum | solution.py:52
  8.8 3.2 %collective-permute-start.1 = (f32[19,1,32,128]{3,2,1,0:T(8,128)S(1)}, f32[19,1,32,128]{3,2,1,0:T(8,128)S(1)}, u32[]{:S(2)}, u32[]{:S(2)}) collective-permute-start(f32[19,1,32,128]{3,2,1,0:T(8,128)S(1)} %get-tuple-element.115), channel_id=1, source_target_pairs={{0,16},{16,32},{32,48},{48,64},{64,80},{80,96},{96,112},{112,128},... | collective-permute-start | bytes 933896 | tf_op jit(solution)/shard_map/ppermute | solution.py:43
  12.0 4.2 %collective-permute-start.3 = (f32[19,1,32,128]{3,2,1,0:T(8,128)S(1)}, f32[19,1,32,128]{3,2,1,0:T(8,128)S(1)}, u32[]{:S(2)}, u32[]{:S(2)}) collective-permute-start(f32[19,1,32,128]{3,2,1,0:T(8,128)S(1)} %get-tuple-element.114), channel_id=1, source_target_pairs={{16,0},{32,16},{48,32},{64,48},{80,64},{96,80},{112,96},{128,112},... | collective-permute-start | bytes 933896 | tf_op jit(solution)/shard_map/ppermute | solution.py:46
  16.2 2.1 %collective-permute-start.2 = (s32[1,32,128]{2,1,0:T(8,128)S(1)}, s32[1,32,128]{2,1,0:T(8,128)S(1)}, u32[]{:S(2)}, u32[]{:S(2)}) collective-permute-start(s32[1,32,128]{2,1,0:T(8,128)S(1)} %get-tuple-element.120), channel_id=1, source_target_pairs={{16,0},{32,16},{48,32},{64,48},{80,64},{96,80},{112,96},{128,112},... | collective-permute-start | bytes 49160 | tf_op jit(solution)/shard_map/ppermute | solution.py:46
  19.0 3.0 %collective-permute-done.2 = s32[1,32,128]{2,1,0:T(8,128)S(1)} collective-permute-done((s32[1,32,128]{2,1,0:T(8,128)S(1)}, s32[1,32,128]{2,1,0:T(8,128)S(1)}, u32[]{:S(2)}, u32[]{:S(2)}) %collective-permute-start.2) | collective-permute-done | bytes 16416 | tf_op jit(solution)/shard_map/ppermute | solution.py:46
  21.9 5.6 %collective-permute-start.4 = (s32[10,1,128]{2,1,0:T(1,128)S(1)}, s32[10,1,128]{2,1,0:T(1,128)S(1)}, u32[]{:S(2)}, u32[]{:S(2)}) collective-permute-start(s32[10,1,128]{2,1,0:T(1,128)S(1)} %get-tuple-element.117), channel_id=1, source_target_pairs={{0,1},{1,2},{2,3},{3,4},{4,5},{5,6},{6,7},{7,8},{8,9},{9,10},{10,1... | collective-permute-start | bytes 15368 | tf_op jit(solution)/shard_map/ppermute | solution.py:43
  27.5 1.9 %collective-permute-start.6 = (s32[10,1,128]{2,1,0:T(1,128)S(1)}, s32[10,1,128]{2,1,0:T(1,128)S(1)}, u32[]{:S(2)}, u32[]{:S(2)}) collective-permute-start(s32[10,1,128]{2,1,0:T(1,128)S(1)} %get-tuple-element.116), channel_id=1, source_target_pairs={{1,0},{2,1},{3,2},{4,3},{5,4},{6,5},{7,6},{8,7},{9,8},{10,9},{11,1... | collective-permute-start | bytes 15368 | tf_op jit(solution)/shard_map/ppermute | solution.py:46
  29.6 3.6 %collective-permute-start.5 = (f32[19,10,1,128]{3,2,1,0:T(1,128)S(1)}, f32[19,10,1,128]{3,2,1,0:T(1,128)S(1)}, u32[]{:S(2)}, u32[]{:S(2)}) collective-permute-start(f32[19,10,1,128]{3,2,1,0:T(1,128)S(1)} %get-tuple-element.109), channel_id=1, source_target_pairs={{0,1},{1,2},{2,3},{3,4},{4,5},{5,6},{6,7},{7,8},{8,9},{9,10},{10,1... | collective-permute-start | bytes 291848 | tf_op jit(solution)/shard_map/ppermute | solution.py:43
  33.3 1.9 %collective-permute-start.7 = (f32[19,10,1,128]{3,2,1,0:T(1,128)S(1)}, f32[19,10,1,128]{3,2,1,0:T(1,128)S(1)}, u32[]{:S(2)}, u32[]{:S(2)}) collective-permute-start(f32[19,10,1,128]{3,2,1,0:T(1,128)S(1)} %get-tuple-element.108), channel_id=1, source_target_pairs={{1,0},{2,1},{3,2},{4,3},{5,4},{6,5},{7,6},{8,7},{9,8},{10,9},{11,1... | collective-permute-start | bytes 291848 | tf_op jit(solution)/shard_map/ppermute | solution.py:46
  35.3 3.9 %collective-permute-done.7 = f32[19,10,1,128]{3,2,1,0:T(1,128)S(1)} collective-permute-done((f32[19,10,1,128]{3,2,1,0:T(1,128)S(1)}, f32[19,10,1,128]{3,2,1,0:T(1,128)S(1)}, u32[]{:S(2)}, u32[]{:S(2)}) %collective-permute-start.7) | collective-permute-done | bytes 97312 | tf_op jit(solution)/shard_map/ppermute | solution.py:46
  39.2 6.7 %select_maximum_fusion.4 = f32[19,10,34,130]{3,2,1,0:T(8,128)S(1)} fusion(f32[19,10,1,128]{3,2,1,0:T(1,128)S(1)} %collective-permute-done.7, f32[19,10,1,128]{3,2,1,0:T(1,128)S(1)} %collective-permute-done.5, f32[19,1,32,128]{3,2,1,0:T(8,128)S(1)} %collective-permute-done.3, f32[19,8,32,128]{3,2,1,0:T(8,128)S(1)} %fusion.139, ...), kind=kLoop, calls=%fused_computation.7 | loop fusion | flops 10077600 | bytes 6666720 | tf_op jit(solution)/shard_map/concatenate | solution.py:47
  45.9 3.8 %bitcast_dynamic-update-slice_fusion.18 = (f32[19,8,32,128]{3,2,1,0:T(8,128)S(1)}, f32[8,32,128]{2,1,0:T(8,128)}, f32[8,32,128]{2,1,0:T(8,128)S(1)}, f32[8,32,12...) fusion(f32[8,32,128]{2,1,0:T(8,128)S(1)} %get-tuple-element.96,, ...), kind=kLoop, calls=%fused_computation.581 | loop fusion | flops 11436031 | bytes 12011520
  49.7 0.8 bitcast_dynamic-update-slice_fusion.17
  51.2 0.7 bitcast_dynamic-update-slice_fusion.15
  51.9 0.8 bitcast_dynamic-update-slice_fusion.14
  53.6 0.7 bitcast_dynamic-update-slice_fusion.10
  54.4 0.8 bitcast_dynamic-update-slice_fusion.9
  55.2 0.7 bitcast_dynamic-update-slice_fusion.8
  56.6 0.7 bitcast_dynamic-update-slice_fusion.6
  57.4 0.7 bitcast_dynamic-update-slice_fusion.5
  58.1 0.8 bitcast_dynamic-update-slice_fusion.4
  58.9 0.8 bitcast_dynamic-update-slice_fusion.3
  59.6 0.8 bitcast_dynamic-update-slice_fusion.2
  60.4 0.8 bitcast_dynamic-update-slice_fusion.1
  61.2 0.8 bitcast_dynamic-update-slice_fusion
  61.9 0.9 fusion.525
  62.8 2.8 %collective-permute-start.8 = (f32[19,1,32,128]{3,2,1,0:T(8,128)}, f32[19,1,32,128]{3,2,1,0:T(8,128)S(1)}, u32[]{:S(2)}, u32[]{:S(2)}) collective-permute-start(f32[19,1,32,128]{3,2,1,0:T(8,128)} %get-tuple-element.113), channel_id=1, source_target_pairs={{0,16},{16,32},{32,48},{48,64},{64,80},{80,96},{96,112},{112,128},... | collective-permute-start | bytes 933896 | tf_op jit(solution)/shard_map/ppermute | solution.py:43
  65.6 5.3 %collective-permute-start.9 = (f32[19,1,32,128]{3,2,1,0:T(8,128)}, f32[19,1,32,128]{3,2,1,0:T(8,128)S(1)}, u32[]{:S(2)}, u32[]{:S(2)}) collective-permute-start(f32[19,1,32,128]{3,2,1,0:T(8,128)} %get-tuple-element.112), channel_id=1, source_target_pairs={{16,0},{32,16},{48,32},{64,48},{80,64},{96,80},{112,96},{128,112},... | collective-permute-start | bytes 933896 | tf_op jit(solution)/shard_map/ppermute | solution.py:46
  70.9 6.6 %stack.76 = f32[1,2,4,8,4,32,4]{6,5,4,3,2,1,0:T(8,128)} reshape(f32[8,32,128]{2,1,0:T(8,128)} %get-tuple-element.119) | data formatting | bytes 262144 | tf_op jit(solution)/shard_map/stack | solution.py:104
  77.7 2.4 %collective-permute-start.10 = (f32[19,10,1,128]{3,2,1,0:T(1,128)S(1)}, f32[19,10,1,128]{3,2,1,0:T(1,128)S(1)}, u32[]{:S(2)}, u32[]{:S(2)}) collective-permute-start(f32[19,10,1,128]{3,2,1,0:T(1,128)S(1)} %get-tuple-element.106), channel_id=1, source_target_pairs={{0,1},{1,2},{2,3},{3,4},{4,5},{5,6},{6,7},{7,8},{8,9},{9,10},{10,1... | collective-permute-start | bytes 291848 | tf_op jit(solution)/shard_map/ppermute | solution.py:43
  80.1 2.1 %collective-permute-start.11 = (f32[19,10,1,128]{3,2,1,0:T(1,128)S(1)}, f32[19,10,1,128]{3,2,1,0:T(1,128)S(1)}, u32[]{:S(2)}, u32[]{:S(2)}) collective-permute-start(f32[19,10,1,128]{3,2,1,0:T(1,128)S(1)} %get-tuple-element.107), channel_id=1, source_target_pairs={{1,0},{2,1},{3,2},{4,3},{5,4},{6,5},{7,6},{8,7},{9,8},{10,9},{11,1... | collective-permute-start | bytes 291848 | tf_op jit(solution)/shard_map/ppermute | solution.py:46
  82.6 3.4 %collective-permute-done.11 = f32[19,10,1,128]{3,2,1,0:T(1,128)S(1)} collective-permute-done((f32[19,10,1,128]{3,2,1,0:T(1,128)S(1)}, f32[19,10,1,128]{3,2,1,0:T(1,128)S(1)}, u32[]{:S(2)}, u32[]{:S(2)}) %collective-permute-start.11) | collective-permute-done | bytes 97312 | tf_op jit(solution)/shard_map/ppermute | solution.py:46
  86.0 6.7 %select_maximum_fusion = f32[19,10,34,130]{3,2,1,0:T(8,128)S(1)} fusion(f32[19,10,1,128]{3,2,1,0:T(1,128)S(1)} %collective-permute-done.11, f32[19,10,1,128]{3,2,1,0:T(1,128)S(1)} %collective-permute-done.10, f32[19,1,32,128]{3,2,1,0:T(8,128)S(1)} %collective-permute-done.9, f32[19,8,32,128]{3,2,1,0:T(8,128)S(1)} %get-tuple-element.18, ...), kind=kLoop, calls=%fused_computation.3 | loop fusion | flops 10077600 | bytes 6666720 | tf_op jit(solution)/shard_map/concatenate | solution.py:47
  93.0 2.1 %divide_multiply_fusion.2 = (f32[8,32,128]{2,1,0:T(8,128)}, f32[8,32,128]{2,1,0:T(8,128)S(1)}, f32[8,32,128]{2,1,0:T(8,128)S(1)}, f32[8,32,128]{2,1,0:T(8,128)S(...) fusion(f32[8,32,128]{2,1,0:T(8,128)S(1)} %get-tuple-element.111, ...), kind=kLoop, calls=%fused_computation.620 | loop fusion | flops 2097152 | bytes 9861120 | tf_op jit(solution)/shard_map/mul | solution.py:105
  95.1 0.9 copy-done.2
  97.1 5.7 %stack.74 = f32[1,2,4,8,4,32,4]{6,5,4,3,2,1,0:T(8,128)} reshape(f32[8,32,128]{2,1,0:T(8,128)S(1)} %divide_multiply_fusion.1) | data formatting | bytes 262144 | tf_op jit(solution)/shard_map/stack | solution.py:104
  102.8 1.3 divide_multiply_fusion
  104.1 5.7 %stack.75 = f32[1,2,4,8,4,32,4]{6,5,4,3,2,1,0:T(8,128)} reshape(f32[8,32,128]{2,1,0:T(8,128)S(1)} %divide_multiply_fusion) | data formatting | bytes 262144 | tf_op jit(solution)/shard_map/stack | solution.py:104
  109.9 5.7 %stack.73 = f32[1,2,4,8,4,32,4]{6,5,4,3,2,1,0:T(8,128)} reshape(f32[8,32,128]{2,1,0:T(8,128)S(1)} %copy-done.29) | data formatting | bytes 262144 | tf_op jit(solution)/shard_map/stack | solution.py:104
  115.5 6.7 %maximum_reduce_fusion = f32[4,2,8,32]{3,2,1,0:T(8,128)S(1)} fusion(f32[1,2,4,8,4,32,4]{6,5,4,3,2,1,0:T(8,128)} %stack.76, f32[1,2,4,8,4,32,4]{6,5,4,3,2,1,0:T(8,128)} %stack.75, f32[1,2,4,8,4,32,4]{6,5,4,3,2,1,0:T(8,128)} %stack.74, f32[1,2,4,8,4,32,4]{6,5,4,3,2,1,0:T(8,128)} %stack.73), kind=kLoop, calls=%fused_computation | loop fusion | flops 522240 | bytes 532480 | tf_op jit(solution)/shard_map/reduce_sum | solution.py:108
  122.6 17.4 %all_to_all.18 = f32[16,1,128]{2,1,0:T(1,128)S(1)} all-to-all(f32[16,1,128]{2,1,0:T(1,128)S(1)} %reshape.129), channel_id=1, replica_groups=mesh['gx'=16,'gy'=16] {'gy'}, dimensions={0} | all-to-all | bytes 16384 | tf_op jit(solution)/shard_map/all_to_all | solution.py:140
  141.7 1.9 %collective-permute-start.12 = (f32[4,1,128,2]{2,3,1,0:T(2,128)S(1)}, f32[4,1,128,2]{2,3,1,0:T(2,128)S(1)}, u32[]{:S(2)}, u32[]{:S(2)}) collective-permute-start(f32[4,1,128,2]{2,3,1,0:T(2,128)S(1)} %get-tuple-element.127), channel_id=1, source_target_pairs={{0,16},{16,32},{32,48},{48,64},{64,80},{80,96},{96,112},{112,128},... | collective-permute-start | bytes 12296 | tf_op jit(solution)/shard_map/ppermute | solution.py:43
  143.6 5.5 %collective-permute-start.13 = (f32[4,1,128,2]{2,3,1,0:T(2,128)S(1)}, f32[4,1,128,2]{2,3,1,0:T(2,128)S(1)}, u32[]{:S(2)}, u32[]{:S(2)}) collective-permute-start(f32[4,1,128,2]{2,3,1,0:T(2,128)S(1)} %get-tuple-element.126), channel_id=1, source_target_pairs={{16,0},{32,16},{48,32},{64,48},{80,64},{96,80},{112,96},{128,112},... | collective-permute-start | bytes 12296 | tf_op jit(solution)/shard_map/ppermute | solution.py:46
  149.8 3.9 %collective-permute-start.14 = (f32[4,4,128,1]{2,3,1,0:T(1,128)S(1)}, f32[4,4,128,1]{2,3,1,0:T(1,128)S(1)}, u32[]{:S(2)}, u32[]{:S(2)}) collective-permute-start(f32[4,4,128,1]{2,3,1,0:T(1,128)S(1)} %get-tuple-element.122), channel_id=1, source_target_pairs={{0,1},{1,2},{2,3},{3,4},{4,5},{5,6},{6,7},{7,8},{8,9},{9,10},{10,1... | collective-permute-start | bytes 24584 | tf_op jit(solution)/shard_map/ppermute | solution.py:43
  153.7 1.9 %collective-permute-start.15 = (f32[4,4,128,1]{2,3,1,0:T(1,128)S(1)}, f32[4,4,128,1]{2,3,1,0:T(1,128)S(1)}, u32[]{:S(2)}, u32[]{:S(2)}) collective-permute-start(f32[4,4,128,1]{2,3,1,0:T(1,128)S(1)} %get-tuple-element.123), channel_id=1, source_target_pairs={{1,0},{2,1},{3,2},{4,3},{5,4},{6,5},{7,6},{8,7},{9,8},{10,9},{11,1... | collective-permute-start | bytes 24584 | tf_op jit(solution)/shard_map/ppermute | solution.py:46
  155.6 3.0 %collective-permute-done.15 = f32[4,4,128,1]{2,3,1,0:T(1,128)S(1)} collective-permute-done((f32[4,4,128,1]{2,3,1,0:T(1,128)S(1)}, f32[4,4,128,1]{2,3,1,0:T(1,128)S(1)}, u32[]{:S(2)}, u32[]{:S(2)}) %collective-permute-start.15) | collective-permute-done | bytes 8224 | tf_op jit(solution)/shard_map/ppermute | solution.py:46
  (173 shorter events, 10.7 us)
Async XLA Ops:
  0.6 6.0 %copy-start.3 = (s32[8,32,128]{2,1,0:T(8,128)S(1)}, s32[8,32,128]{2,1,0:T(8,128)}, u32[]{:S(2)}) copy-start(s32[8,32,128]{2,1,0:T(8,128)} %param.3) | copy-start | bytes 393220
  1.5 16.7 %collective-permute-start = (s32[1,32,128]{2,1,0:T(8,128)S(1)}, s32[1,32,128]{2,1,0:T(8,128)S(1)}, u32[]{:S(2)}, u32[]{:S(2)}) collective-permute-start(s32[1,32,128]{2,1,0:T(8,128)S(1)} %get-tuple-element.121), channel_id=1, source_target_pairs={{0,16},{16,32},{32,48},{48,64},{64,80},{80,96},{96,112},{112,128},... | collective-permute-start | bytes 49160 | tf_op jit(solution)/shard_map/ppermute | solution.py:43
  8.8 20.7 %collective-permute-start.1 = (f32[19,1,32,128]{3,2,1,0:T(8,128)S(1)}, f32[19,1,32,128]{3,2,1,0:T(8,128)S(1)}, u32[]{:S(2)}, u32[]{:S(2)}) collective-permute-start(f32[19,1,32,128]{3,2,1,0:T(8,128)S(1)} %get-tuple-element.115), channel_id=1, source_target_pairs={{0,16},{16,32},{32,48},{48,64},{64,80},{80,96},{96,112},{112,128},... | collective-permute-start | bytes 933896 | tf_op jit(solution)/shard_map/ppermute | solution.py:43
  12.0 17.5 %collective-permute-start.3 = (f32[19,1,32,128]{3,2,1,0:T(8,128)S(1)}, f32[19,1,32,128]{3,2,1,0:T(8,128)S(1)}, u32[]{:S(2)}, u32[]{:S(2)}) collective-permute-start(f32[19,1,32,128]{3,2,1,0:T(8,128)S(1)} %get-tuple-element.114), channel_id=1, source_target_pairs={{16,0},{32,16},{48,32},{64,48},{80,64},{96,80},{112,96},{128,112},... | collective-permute-start | bytes 933896 | tf_op jit(solution)/shard_map/ppermute | solution.py:46
  16.2 5.7 %collective-permute-start.2 = (s32[1,32,128]{2,1,0:T(8,128)S(1)}, s32[1,32,128]{2,1,0:T(8,128)S(1)}, u32[]{:S(2)}, u32[]{:S(2)}) collective-permute-start(s32[1,32,128]{2,1,0:T(8,128)S(1)} %get-tuple-element.120), channel_id=1, source_target_pairs={{16,0},{32,16},{48,32},{64,48},{80,64},{96,80},{112,96},{128,112},... | collective-permute-start | bytes 49160 | tf_op jit(solution)/shard_map/ppermute | solution.py:46
  21.9 13.3 %collective-permute-start.4 = (s32[10,1,128]{2,1,0:T(1,128)S(1)}, s32[10,1,128]{2,1,0:T(1,128)S(1)}, u32[]{:S(2)}, u32[]{:S(2)}) collective-permute-start(s32[10,1,128]{2,1,0:T(1,128)S(1)} %get-tuple-element.117), channel_id=1, source_target_pairs={{0,1},{1,2},{2,3},{3,4},{4,5},{5,6},{6,7},{7,8},{8,9},{9,10},{10,1... | collective-permute-start | bytes 15368 | tf_op jit(solution)/shard_map/ppermute | solution.py:43
  27.5 7.7 %collective-permute-start.6 = (s32[10,1,128]{2,1,0:T(1,128)S(1)}, s32[10,1,128]{2,1,0:T(1,128)S(1)}, u32[]{:S(2)}, u32[]{:S(2)}) collective-permute-start(s32[10,1,128]{2,1,0:T(1,128)S(1)} %get-tuple-element.116), channel_id=1, source_target_pairs={{1,0},{2,1},{3,2},{4,3},{5,4},{6,5},{7,6},{8,7},{9,8},{10,9},{11,1... | collective-permute-start | bytes 15368 | tf_op jit(solution)/shard_map/ppermute | solution.py:46
  29.6 5.6 %collective-permute-start.5 = (f32[19,10,1,128]{3,2,1,0:T(1,128)S(1)}, f32[19,10,1,128]{3,2,1,0:T(1,128)S(1)}, u32[]{:S(2)}, u32[]{:S(2)}) collective-permute-start(f32[19,10,1,128]{3,2,1,0:T(1,128)S(1)} %get-tuple-element.109), channel_id=1, source_target_pairs={{0,1},{1,2},{2,3},{3,4},{4,5},{5,6},{6,7},{7,8},{8,9},{9,10},{10,1... | collective-permute-start | bytes 291848 | tf_op jit(solution)/shard_map/ppermute | solution.py:43
  33.3 5.9 %collective-permute-start.7 = (f32[19,10,1,128]{3,2,1,0:T(1,128)S(1)}, f32[19,10,1,128]{3,2,1,0:T(1,128)S(1)}, u32[]{:S(2)}, u32[]{:S(2)}) collective-permute-start(f32[19,10,1,128]{3,2,1,0:T(1,128)S(1)} %get-tuple-element.108), channel_id=1, source_target_pairs={{1,0},{2,1},{3,2},{4,3},{5,4},{6,5},{7,6},{8,7},{9,8},{10,9},{11,1... | collective-permute-start | bytes 291848 | tf_op jit(solution)/shard_map/ppermute | solution.py:46
  35.3 10.7 %copy-start.1 = (f32[19,8,32,128]{3,2,1,0:T(8,128)S(1)}, f32[19,8,32,128]{3,2,1,0:T(8,128)}, u32[]{:S(2)}) copy-start(f32[19,8,32,128]{3,2,1,0:T(8,128)} %param.2) | copy-start | bytes 7471108
  62.8 14.7 %collective-permute-start.8 = (f32[19,1,32,128]{3,2,1,0:T(8,128)}, f32[19,1,32,128]{3,2,1,0:T(8,128)S(1)}, u32[]{:S(2)}, u32[]{:S(2)}) collective-permute-start(f32[19,1,32,128]{3,2,1,0:T(8,128)} %get-tuple-element.113), channel_id=1, source_target_pairs={{0,16},{16,32},{32,48},{48,64},{64,80},{80,96},{96,112},{112,128},... | collective-permute-start | bytes 933896 | tf_op jit(solution)/shard_map/ppermute | solution.py:43
  65.6 11.9 %collective-permute-start.9 = (f32[19,1,32,128]{3,2,1,0:T(8,128)}, f32[19,1,32,128]{3,2,1,0:T(8,128)S(1)}, u32[]{:S(2)}, u32[]{:S(2)}) collective-permute-start(f32[19,1,32,128]{3,2,1,0:T(8,128)} %get-tuple-element.112), channel_id=1, source_target_pairs={{16,0},{32,16},{48,32},{64,48},{80,64},{96,80},{112,96},{128,112},... | collective-permute-start | bytes 933896 | tf_op jit(solution)/shard_map/ppermute | solution.py:46
  77.7 4.9 %collective-permute-start.10 = (f32[19,10,1,128]{3,2,1,0:T(1,128)S(1)}, f32[19,10,1,128]{3,2,1,0:T(1,128)S(1)}, u32[]{:S(2)}, u32[]{:S(2)}) collective-permute-start(f32[19,10,1,128]{3,2,1,0:T(1,128)S(1)} %get-tuple-element.106), channel_id=1, source_target_pairs={{0,1},{1,2},{2,3},{3,4},{4,5},{5,6},{6,7},{7,8},{8,9},{9,10},{10,1... | collective-permute-start | bytes 291848 | tf_op jit(solution)/shard_map/ppermute | solution.py:43
  80.1 5.9 %collective-permute-start.11 = (f32[19,10,1,128]{3,2,1,0:T(1,128)S(1)}, f32[19,10,1,128]{3,2,1,0:T(1,128)S(1)}, u32[]{:S(2)}, u32[]{:S(2)}) collective-permute-start(f32[19,10,1,128]{3,2,1,0:T(1,128)S(1)} %get-tuple-element.107), channel_id=1, source_target_pairs={{1,0},{2,1},{3,2},{4,3},{5,4},{6,5},{7,6},{8,7},{9,8},{10,9},{11,1... | collective-permute-start | bytes 291848 | tf_op jit(solution)/shard_map/ppermute | solution.py:46
  82.3 10.4 %copy-start.14 = (f32[8,32,128]{2,1,0:T(8,128)S(1)}, f32[8,32,128]{2,1,0:T(8,128)}, u32[]{:S(2)}) copy-start(f32[8,32,128]{2,1,0:T(8,128)} %get-tuple-element.55) | copy-start | bytes 393220
  82.3 10.4 %copy-start.15 = (f32[8,32,128]{2,1,0:T(8,128)S(1)}, f32[8,32,128]{2,1,0:T(8,128)}, u32[]{:S(2)}) copy-start(f32[8,32,128]{2,1,0:T(8,128)} %get-tuple-element.49) | copy-start | bytes 393220
  82.3 10.4 %copy-start.16 = (f32[8,32,128]{2,1,0:T(8,128)S(1)}, f32[8,32,128]{2,1,0:T(8,128)}, u32[]{:S(2)}) copy-start(f32[8,32,128]{2,1,0:T(8,128)} %get-tuple-element.47) | copy-start | bytes 393220
  82.3 10.4 %copy-start.17 = (f32[8,32,128]{2,1,0:T(8,128)S(1)}, f32[8,32,128]{2,1,0:T(8,128)}, u32[]{:S(2)}) copy-start(f32[8,32,128]{2,1,0:T(8,128)} %get-tuple-element.41) | copy-start | bytes 393220
  82.3 10.4 %copy-start.18 = (f32[8,32,128]{2,1,0:T(8,128)S(1)}, f32[8,32,128]{2,1,0:T(8,128)}, u32[]{:S(2)}) copy-start(f32[8,32,128]{2,1,0:T(8,128)} %get-tuple-element.39) | copy-start | bytes 393220
  82.3 10.4 %copy-start.19 = (f32[8,32,128]{2,1,0:T(8,128)S(1)}, f32[8,32,128]{2,1,0:T(8,128)}, u32[]{:S(2)}) copy-start(f32[8,32,128]{2,1,0:T(8,128)} %get-tuple-element.37) | copy-start | bytes 393220
  82.4 10.4 %copy-start.20 = (f32[8,32,128]{2,1,0:T(8,128)S(1)}, f32[8,32,128]{2,1,0:T(8,128)}, u32[]{:S(2)}) copy-start(f32[8,32,128]{2,1,0:T(8,128)} %get-tuple-element.35) | copy-start | bytes 393220
  82.4 10.4 %copy-start.21 = (f32[8,32,128]{2,1,0:T(8,128)S(1)}, f32[8,32,128]{2,1,0:T(8,128)}, u32[]{:S(2)}) copy-start(f32[8,32,128]{2,1,0:T(8,128)} %get-tuple-element.33) | copy-start | bytes 393220
  82.4 10.4 %copy-start.22 = (f32[8,32,128]{2,1,0:T(8,128)S(1)}, f32[8,32,128]{2,1,0:T(8,128)}, u32[]{:S(2)}) copy-start(f32[8,32,128]{2,1,0:T(8,128)} %get-tuple-element.31) | copy-start | bytes 393220
  82.4 10.4 %copy-start.23 = (f32[8,32,128]{2,1,0:T(8,128)S(1)}, f32[8,32,128]{2,1,0:T(8,128)}, u32[]{:S(2)}) copy-start(f32[8,32,128]{2,1,0:T(8,128)} %get-tuple-element.29) | copy-start | bytes 393220
  82.4 10.4 %copy-start.24 = (f32[8,32,128]{2,1,0:T(8,128)S(1)}, f32[8,32,128]{2,1,0:T(8,128)}, u32[]{:S(2)}) copy-start(f32[8,32,128]{2,1,0:T(8,128)} %get-tuple-element.27) | copy-start | bytes 393220
  82.4 10.4 %copy-start.25 = (f32[8,32,128]{2,1,0:T(8,128)S(1)}, f32[8,32,128]{2,1,0:T(8,128)}, u32[]{:S(2)}) copy-start(f32[8,32,128]{2,1,0:T(8,128)} %get-tuple-element.25) | copy-start | bytes 393220
  82.4 10.4 %copy-start.26 = (f32[8,32,128]{2,1,0:T(8,128)S(1)}, f32[8,32,128]{2,1,0:T(8,128)}, u32[]{:S(2)}) copy-start(f32[8,32,128]{2,1,0:T(8,128)} %get-tuple-element.23) | copy-start | bytes 393220
  82.4 10.4 %copy-start.27 = (f32[8,32,128]{2,1,0:T(8,128)S(1)}, f32[8,32,128]{2,1,0:T(8,128)}, u32[]{:S(2)}) copy-start(f32[8,32,128]{2,1,0:T(8,128)} %get-tuple-element.21) | copy-start | bytes 393220
  82.4 10.4 %copy-start.28 = (f32[8,32,128]{2,1,0:T(8,128)S(1)}, f32[8,32,128]{2,1,0:T(8,128)}, u32[]{:S(2)}) copy-start(f32[8,32,128]{2,1,0:T(8,128)} %get-tuple-element.19) | copy-start | bytes 393220
  82.4 10.4 %copy-start.36 = (pred[8,32,128]{2,1,0:T(8,128)(4,1)S(1)}, pred[8,32,128]{2,1,0:T(8,128)(4,1)}, u32[]{:S(2)}) copy-start(pred[8,32,128]{2,1,0:T(8,128)(4,1)} %get-tuple-element.71) | copy-start | bytes 98308
  82.5 10.4 %copy-start.38 = (pred[8,32,128]{2,1,0:T(8,128)(4,1)S(1)}, pred[8,32,128]{2,1,0:T(8,128)(4,1)}, u32[]{:S(2)}) copy-start(pred[8,32,128]{2,1,0:T(8,128)(4,1)} %get-tuple-element.65) | copy-start | bytes 98308
  82.5 10.4 %copy-start.39 = (pred[8,32,128]{2,1,0:T(8,128)(4,1)S(1)}, pred[8,32,128]{2,1,0:T(8,128)(4,1)}, u32[]{:S(2)}) copy-start(pred[8,32,128]{2,1,0:T(8,128)(4,1)} %get-tuple-element.67) | copy-start | bytes 98308
  82.5 10.4 %copy-start.40 = (pred[8,32,128]{2,1,0:T(8,128)(4,1)S(1)}, pred[8,32,128]{2,1,0:T(8,128)(4,1)}, u32[]{:S(2)}) copy-start(pred[8,32,128]{2,1,0:T(8,128)(4,1)} %get-tuple-element.73) | copy-start | bytes 98308
  82.5 10.4 %copy-start.41 = (pred[8,32,128]{2,1,0:T(8,128)(4,1)S(1)}, pred[8,32,128]{2,1,0:T(8,128)(4,1)}, u32[]{:S(2)}) copy-start(pred[8,32,128]{2,1,0:T(8,128)(4,1)} %get-tuple-element.75) | copy-start | bytes 98308
  82.5 10.4 %copy-start.42 = (pred[8,32,128]{2,1,0:T(8,128)(4,1)S(1)}, pred[8,32,128]{2,1,0:T(8,128)(4,1)}, u32[]{:S(2)}) copy-start(pred[8,32,128]{2,1,0:T(8,128)(4,1)} %get-tuple-element.77) | copy-start | bytes 98308
  82.5 10.4 %copy-start.43 = (pred[8,32,128]{2,1,0:T(8,128)(4,1)S(1)}, pred[8,32,128]{2,1,0:T(8,128)(4,1)}, u32[]{:S(2)}) copy-start(pred[8,32,128]{2,1,0:T(8,128)(4,1)} %get-tuple-element.79) | copy-start | bytes 98308
  82.5 10.4 %copy-start.44 = (pred[8,32,128]{2,1,0:T(8,128)(4,1)S(1)}, pred[8,32,128]{2,1,0:T(8,128)(4,1)}, u32[]{:S(2)}) copy-start(pred[8,32,128]{2,1,0:T(8,128)(4,1)} %get-tuple-element.81) | copy-start | bytes 98308
  82.5 10.4 %copy-start.45 = (pred[8,32,128]{2,1,0:T(8,128)(4,1)S(1)}, pred[8,32,128]{2,1,0:T(8,128)(4,1)}, u32[]{:S(2)}) copy-start(pred[8,32,128]{2,1,0:T(8,128)(4,1)} %get-tuple-element.83) | copy-start | bytes 98308
  82.5 10.4 %copy-start.46 = (pred[8,32,128]{2,1,0:T(8,128)(4,1)S(1)}, pred[8,32,128]{2,1,0:T(8,128)(4,1)}, u32[]{:S(2)}) copy-start(pred[8,32,128]{2,1,0:T(8,128)(4,1)} %get-tuple-element.85) | copy-start | bytes 98308
  82.5 10.4 %copy-start.47 = (pred[8,32,128]{2,1,0:T(8,128)(4,1)S(1)}, pred[8,32,128]{2,1,0:T(8,128)(4,1)}, u32[]{:S(2)}) copy-start(pred[8,32,128]{2,1,0:T(8,128)(4,1)} %get-tuple-element.87) | copy-start | bytes 98308
  82.6 10.4 %copy-start.48 = (pred[8,32,128]{2,1,0:T(8,128)(4,1)S(1)}, pred[8,32,128]{2,1,0:T(8,128)(4,1)}, u32[]{:S(2)}) copy-start(pred[8,32,128]{2,1,0:T(8,128)(4,1)} %get-tuple-element.89) | copy-start | bytes 98308
  82.6 10.4 %copy-start.49 = (pred[8,32,128]{2,1,0:T(8,128)(4,1)S(1)}, pred[8,32,128]{2,1,0:T(8,128)(4,1)}, u32[]{:S(2)}) copy-start(pred[8,32,128]{2,1,0:T(8,128)(4,1)} %get-tuple-element.91) | copy-start | bytes 98308
  82.6 10.4 %copy-start.50 = (pred[8,32,128]{2,1,0:T(8,128)(4,1)S(1)}, pred[8,32,128]{2,1,0:T(8,128)(4,1)}, u32[]{:S(2)}) copy-start(pred[8,32,128]{2,1,0:T(8,128)(4,1)} %get-tuple-element.94) | copy-start | bytes 98308
  82.6 10.4 %copy-start.51 = (pred[8,32,128]{2,1,0:T(8,128)(4,1)S(1)}, pred[8,32,128]{2,1,0:T(8,128)(4,1)}, u32[]{:S(2)}) copy-start(pred[8,32,128]{2,1,0:T(8,128)(4,1)} %get-tuple-element.95) | copy-start | bytes 98308
  141.7 7.4 %collective-permute-start.12 = (f32[4,1,128,2]{2,3,1,0:T(2,128)S(1)}, f32[4,1,128,2]{2,3,1,0:T(2,128)S(1)}, u32[]{:S(2)}, u32[]{:S(2)}) collective-permute-start(f32[4,1,128,2]{2,3,1,0:T(2,128)S(1)} %get-tuple-element.127), channel_id=1, source_target_pairs={{0,16},{16,32},{32,48},{48,64},{64,80},{80,96},{96,112},{112,128},... | collective-permute-start | bytes 12296 | tf_op jit(solution)/shard_map/ppermute | solution.py:43
  143.6 6.2 %collective-permute-start.13 = (f32[4,1,128,2]{2,3,1,0:T(2,128)S(1)}, f32[4,1,128,2]{2,3,1,0:T(2,128)S(1)}, u32[]{:S(2)}, u32[]{:S(2)}) collective-permute-start(f32[4,1,128,2]{2,3,1,0:T(2,128)S(1)} %get-tuple-element.126), channel_id=1, source_target_pairs={{16,0},{32,16},{48,32},{64,48},{80,64},{96,80},{112,96},{128,112},... | collective-permute-start | bytes 12296 | tf_op jit(solution)/shard_map/ppermute | solution.py:46
  149.8 5.8 %collective-permute-start.14 = (f32[4,4,128,1]{2,3,1,0:T(1,128)S(1)}, f32[4,4,128,1]{2,3,1,0:T(1,128)S(1)}, u32[]{:S(2)}, u32[]{:S(2)}) collective-permute-start(f32[4,4,128,1]{2,3,1,0:T(1,128)S(1)} %get-tuple-element.122), channel_id=1, source_target_pairs={{0,1},{1,2},{2,3},{3,4},{4,5},{5,6},{6,7},{7,8},{8,9},{9,10},{10,1... | collective-permute-start | bytes 24584 | tf_op jit(solution)/shard_map/ppermute | solution.py:43
  153.7 5.0 %collective-permute-start.15 = (f32[4,4,128,1]{2,3,1,0:T(1,128)S(1)}, f32[4,4,128,1]{2,3,1,0:T(1,128)S(1)}, u32[]{:S(2)}, u32[]{:S(2)}) collective-permute-start(f32[4,4,128,1]{2,3,1,0:T(1,128)S(1)} %get-tuple-element.123), channel_id=1, source_target_pairs={{1,0},{2,1},{3,2},{4,3},{5,4},{6,5},{7,6},{8,7},{9,8},{10,9},{11,1... | collective-permute-start | bytes 24584 | tf_op jit(solution)/shard_map/ppermute | solution.py:46
  (22 other events, 95.0 us)
where the time goes:
time: 162 us; the launch traced here: 160 us
  starting transfers between devices  51.5 us (32%)
  other arithmetic  46.5 us (29%)
  local copies, waits for them, and re-layouts  28.7 us (18%)
  blocking collectives  17.4 us (11%)
  waiting for transfers between devices  14 us (9%)
  between operations  1.82 us (1%)
    ppermute x8, starting transfers between devices, extended_2(): lax.ppermute(lax.slice_in_dim(block, block.shape[dim] - width, None, axis...  26.6 us
    ppermute x8, starting transfers between devices, extended_2(): lax.ppermute(lax.slice_in_dim(block, 0, width, axis=dim), axis, backward)  25 us
    another operation x4, local copies, waits for them, and re-layouts, voxel_sums(): jnp.stack([fluid_float * speed_x, fluid_float * speed_y, fluid_float * sp...  23.6 us
    unnamed x36, other arithmetic  17.4 us
    all_to_all x1, blocking collectives, local(): moved = lax.all_to_all(sums, 'gy', split_axis=3, concat_axis=2, tiled=True)  17.4 us
    ppermute x8, waiting for transfers between devices, extended_2(): lax.ppermute(lax.slice_in_dim(block, 0, width, axis=dim), axis, backward)  14 us
    concatenate x5, other arithmetic, extended_2(): block = jnp.concatenate([low, block, high], axis=dim)  13.6 us
    reduce_sum x1, other arithmetic, voxel_sums(): stacked.reshape(4, size_x // 4, 4, size_y // 4, 4, size_z // 4, 4)  6.74 us
  transfers between devices with their start and end apart: 16, of which 5 were waited for; matrix products, arithmetic and copies ran while one was open for 7% of the time, Pallas kernels for 0%

commit v1 on v0

v1 whole, which is shorter than its diff:
```python
import functools

import jax
import jax.numpy as jnp
from jax import lax
from jax.experimental import pallas as pl
from jax.experimental.pallas import tpu as pltpu
from jax.sharding import PartitionSpec as P

MESH = pl.DeviceIdType.MESH

VELOCITIES = (
    (0, 0, 0),
    (1, 0, 0),
    (-1, 0, 0),
    (0, 1, 0),
    (0, -1, 0),
    (0, 0, 1),
    (0, 0, -1),
    (1, 1, 0),
    (-1, -1, 0),
    (1, -1, 0),
    (-1, 1, 0),
    (1, 0, 1),
    (-1, 0, -1),
    (1, 0, -1),
    (-1, 0, 1),
    (0, 1, 1),
    (0, -1, -1),
    (0, 1, -1),
    (0, -1, 1),
)
OPPOSITE = (0, 2, 1, 4, 3, 6, 5, 8, 7, 10, 9, 12, 11, 14, 13, 16, 15, 18, 17)
ORDER = (9, 1, 11, 13, 7, 3, 15, 17, 10, 2, 14, 12, 8, 4, 18, 16, 0, 5, 6)
SLOT = tuple(ORDER.index(channel) for channel in range(19))
relax_rate = 1.0 / 0.6
velocity_scale = 0.002

NX, NY, NZ = 8, 32, 128
TOP = 8
LAST = TOP + NY - 1
TILES = NY // 8


def moments(f):
    s = [f[i] + f[i + 1] for i in range(1, 19, 2)]
    d = [f[i] - f[i + 1] for i in range(1, 19, 2)]
    rho = (f[0] + s[8]) + ((s[0] + s[1]) + (s[2] + s[3])) + ((s[4] + s[5]) + (s[6] + s[7]))
    mx = d[0] + (d[3] + d[4]) + (d[5] + d[6])
    my = d[1] + (d[3] - d[4]) + (d[7] + d[8])
    mz = d[2] + (d[5] - d[6]) + (d[7] - d[8])
    return rho, mx, my, mz


def collide(f):
    rho, mx, my, mz = moments(f)
    inverse = 1.0 / rho
    ux, uy, uz = mx * inverse, my * inverse, mz * inverse
    base = rho - 1.5 * (mx * ux + my * uy + mz * uz)
    keep = 1.0 - relax_rate
    relaxed = [keep * f[0] + (relax_rate / 3.0) * base]
    vx, vy, vz = 1.5 * ux, 1.5 * uy, 1.5 * uz
    near = (relax_rate / 18.0) * base
    far = (relax_rate / 36.0) * base
    ax, ay, az = (relax_rate / 6.0) * mx, (relax_rate / 6.0) * my, (relax_rate / 6.0) * mz
    bx, by, bz = 0.5 * ax, 0.5 * ay, 0.5 * az
    for channel, level, flow, speed in (
        (1, near, ax, vx),
        (3, near, ay, vy),
        (5, near, az, vz),
        (7, far, bx + by, vx + vy),
        (9, far, bx - by, vx - vy),
        (11, far, bx + bz, vx + vz),
        (13, far, bx - bz, vx - vz),
        (15, far, by + bz, vy + vz),
        (17, far, by - bz, vy - vz),
    ):
        even = level + flow * speed
        relaxed.append(keep * f[channel] + (even + flow))
        relaxed.append(keep * f[channel + 1] + (even - flow))
    return relaxed


def pulled(held, walls, x, tile):
    f = []
    for channel in range(19):
        cx, cy, cz = VELOCITIES[channel]
        rows = pl.ds(TOP + 8 * tile, 8)
        if channel == 0:
            f.append(held[SLOT[0], x + 1, rows, :])
            continue
        from_rows = pl.ds(TOP + 8 * tile - cy, 8)
        source = held[SLOT[channel], x + 1 - cx, from_rows, :]
        if cz:
            source = pltpu.roll(source, cz % NZ, 1)
        open_site = walls[cz % 3, x + 1 - cx, from_rows, :]
        f.append(jnp.where(open_site > 0, source, held[SLOT[OPPOSITE[channel]], x + 1, rows, :]))
    return f


def kernel(
    gx_size,
    gy_size,
    populations,
    fluid,
    velocity_ref,
    magnitude_ref,
    start,
    first,
    second,
    walls,
    sums,
    zmat,
    ymat,
    table,
    beside,
    mixed,
    gathered,
    final,
    load_sem,
    fluid_sem,
    flag_send,
    flag_recv,
    halo_send,
    halo_recv,
    side_send,
    side_recv,
    all_send,
    all_recv,
):
    gx, gy = lax.axis_index("gx"), lax.axis_index("gy")
    right, left = lax.rem(gx + 1, gx_size), lax.rem(gx + gx_size - 1, gx_size)
    above, below = lax.rem(gy + 1, gy_size), lax.rem(gy + gy_size - 1, gy_size)

    fluid_copy = pltpu.make_async_copy(fluid, walls.at[0, pl.ds(1, NX), pl.ds(TOP, NY), :], fluid_sem)
    fluid_copy.start()

    def load(x):
        return pltpu.make_async_copy(populations.at[:, x], start.at[:, x], load_sem.at[x])

    load_order = (7, 0, 1, 2, 3, 4, 5, 6)
    for x in load_order:
        load(x).start()

    barrier = pltpu.get_barrier_semaphore()
    greeted = [(a, b) for a in (left, gx, right) for b in (below, gy, above) if not (a is gx and b is gy)]
    for target in greeted:
        pl.semaphore_signal(barrier, inc=1, device_id=target, device_id_type=MESH)

    def greet(step, carry):
        pl.semaphore_signal(
            barrier, inc=1, device_id=(gx, lax.rem(gy + step, gy_size)), device_id_type=MESH
        )
        return carry

    lax.fori_loop(2, gy_size - 1, greet, 0)

    def lane_walls(slab, rows):
        flags = walls[0, slab, rows, :]
        lane = lax.broadcasted_iota(jnp.int32, flags.shape, flags.ndim - 1)
        walls[1, slab, rows, :] = jnp.where(lane == 0, 0, pltpu.roll(flags, 1, flags.ndim - 1))
        walls[2, slab, rows, :] = jnp.where(lane == NZ - 1, 0, pltpu.roll(flags, NZ - 1, flags.ndim - 1))

    row = lax.broadcasted_iota(jnp.int32, (32, NZ), 0)
    lane = lax.broadcasted_iota(jnp.int32, (32, NZ), 1)
    distance = jnp.abs(2 * (row % 16) + row // 16 - lane // 4)
    zmat[...] = jnp.where(distance == 0, 0.5, jnp.where(distance == 1, 0.25, 0.0)).astype(jnp.float32)

    def y_rows(step, carry):
        at = pl.multiple_of(8 * step, 8)
        row = lax.broadcasted_iota(jnp.int32, (8, 128), 0) + at
        lane = lax.broadcasted_iota(jnp.int32, (8, 128), 1)
        for z in range(2):
            hit = (row // 32 == 7 - lane // 16) & ((row % 32) // 4 == lane % 8) & ((lane // 8) % 2 == 1 - z)
            ymat[z, pl.ds(at, 8), :] = jnp.where(hit, 1.0, 0.0).astype(jnp.float32)
        return carry

    lax.fori_loop(0, 32, y_rows, 0)
    sums[...] = jnp.zeros(sums.shape, jnp.float32)

    fluid_copy.wait()

    def wall_slab(slab, carry):
        for tile in range(TILES):
            lane_walls(slab, pl.ds(TOP + 8 * tile, 8))
        return carry

    lax.fori_loop(1, NX + 1, wall_slab, 0)

    pl.semaphore_wait(barrier, 8 + gy_size - 3)

    def remote(buffer, source, target, send, recv, device):
        return pltpu.make_async_remote_copy(
            src_ref=buffer.at[source],
            dst_ref=buffer.at[target],
            send_sem=send,
            recv_sem=recv,
            device_id=device,
            device_id_type=MESH,
        )

    inner, block = pl.ds(1, NX), pl.ds(TOP, NY)
    low, high = pl.ds(TOP - 1, 1), pl.ds(LAST + 1, 1)
    bottom, top = pl.ds(TOP, 1), pl.ds(LAST, 1)

    def sides():
        x_faces = [
            (pl.ds(0, 5), (NX, block), (0, block), (right, gy)),
            (pl.ds(8, 5), (1, block), (NX + 1, block), (left, gy)),
            (pl.ds(4, 1), (NX, top), (0, low), (right, above)),
            (pl.ds(0, 1), (NX, bottom), (0, high), (right, below)),
            (pl.ds(8, 1), (1, top), (NX + 1, low), (left, above)),
            (pl.ds(12, 1), (1, bottom), (NX + 1, high), (left, below)),
        ]
        y_faces = [
            (pl.ds(4, 5), (inner, top), (inner, low), (gx, above)),
            (pl.ds(12, 4), (inner, bottom), (inner, high), (gx, below)),
            (pl.ds(0, 1), (inner, bottom), (inner, high), (gx, below)),
        ]
        return x_faces, y_faces

    x_faces, y_faces = sides()
    flags = [
        remote(walls, (0, *s), (0, *t), flag_send.at[i], flag_recv.at[i], device)
        for i, (_, s, t, device) in enumerate(x_faces + y_faces[:2])
    ]
    for copy in flags:
        copy.start()

    def halo(buffer, which):
        copies = [
            remote(buffer, (slots, *s), (slots, *t), halo_send.at[which, i], halo_recv.at[which, i], device)
            for i, (slots, s, t, device) in enumerate(x_faces + y_faces)
        ]
        return copies[:6], copies[6:]

    first_x, first_y = halo(first, 0)
    second_x, second_y = halo(second, 1)

    def relax_tile(x, tile):
        rows = pl.ds(8 * tile, 8)
        relaxed = collide([start[channel, x, rows, :] for channel in range(19)])
        for channel in range(19):
            first[SLOT[channel], x + 1, pl.ds(TOP + 8 * tile, 8), :] = relaxed[channel]

    def step_tile(x, tile):
        relaxed = collide(pulled(first, walls, x, tile))
        for channel in range(19):
            second[SLOT[channel], x + 1, pl.ds(TOP + 8 * tile, 8), :] = relaxed[channel]

    def sum_tile(x, tile):
        rho, mx, my, mz = moments(pulled(second, walls, x, tile))
        here = walls[0, x + 1, pl.ds(TOP + 8 * tile, 8), :].astype(jnp.float32)
        scale = here / rho
        for component, value in enumerate((mx * scale, my * scale, mz * scale, here)):
            rows = pl.ds(pl.multiple_of(component * 64 + (x // 4) * 32 + 8 * tile, 8), 8)
            sums[rows, :] = sums[rows, :] + value

    def over_slabs(body, edge, tiles):
        def edge_slab(step, carry):
            for tile in tiles:
                body((NX - 1) * (1 - step), tile)
            return carry

        def inner_slab(x, carry):
            for tile in tiles:
                body(x, tile)
            return carry

        if edge:
            lax.fori_loop(0, 2, edge_slab, 0)
        else:
            lax.fori_loop(1, NX - 1, inner_slab, 0)

    every, outer, middle = range(TILES), (0, TILES - 1), range(1, TILES - 1)

    load(7).wait()
    load(0).wait()
    over_slabs(relax_tile, True, every)
    for copy in first_x:
        copy.start()
    for x in range(1, NX - 1):
        load(x).wait()
    over_slabs(relax_tile, False, outer)
    for copy in first_y:
        copy.start()
    over_slabs(relax_tile, False, middle)

    over_slabs(step_tile, False, middle)

    for copy in flags:
        copy.wait_recv()

    @pl.when(gx == 0)
    def _():
        walls[0, 0, pl.ds(TOP - 1, NY + 2), :] = jnp.zeros((NY + 2, NZ), jnp.int32)

    @pl.when(gx == gx_size - 1)
    def _():
        walls[0, NX + 1, pl.ds(TOP - 1, NY + 2), :] = jnp.zeros((NY + 2, NZ), jnp.int32)

    @pl.when(gy == 0)
    def _():
        walls[0, :, low, :] = jnp.zeros((NX + 2, 1, NZ), jnp.int32)

    @pl.when(gy == gy_size - 1)
    def _():
        walls[0, :, high, :] = jnp.zeros((NX + 2, 1, NZ), jnp.int32)

    for slab in (0, NX + 1):
        wall_slab(slab, 0)

    def wall_rows(slab, carry):
        lane_walls(slab, low)
        lane_walls(slab, high)
        return carry

    lax.fori_loop(0, NX + 2, wall_rows, 0)

    for copy in first_x + first_y:
        copy.wait_recv()
    over_slabs(step_tile, True, every)
    for copy in second_x:
        copy.start()
    over_slabs(step_tile, False, outer)
    for copy in second_y:
        copy.start()

    over_slabs(sum_tile, False, middle)
    for copy in second_x + second_y:
        copy.wait_recv()
    over_slabs(sum_tile, True, every)
    over_slabs(sum_tile, False, outer)

    exact = dict(preferred_element_type=jnp.float32, precision=lax.Precision.HIGHEST)
    blurred_z = lax.dot_general(zmat[...], sums[...], (((1,), (1,)), ((), ())), **exact)
    table[...] = jnp.dot(blurred_z[:16], ymat[0], **exact) + jnp.dot(blurred_z[16:], ymat[1], **exact)

    to_right = pltpu.make_async_remote_copy(
        src_ref=table,
        dst_ref=beside.at[0],
        send_sem=side_send.at[0],
        recv_sem=side_recv.at[0],
        device_id=(right, gy),
        device_id_type=MESH,
    )
    to_left = pltpu.make_async_remote_copy(
        src_ref=table,
        dst_ref=beside.at[1],
        send_sem=side_send.at[1],
        recv_sem=side_recv.at[1],
        device_id=(left, gy),
        device_id_type=MESH,
    )
    to_right.start()
    to_left.start()
    to_right.wait_recv()
    to_left.wait_recv()
    own = table[...]
    lane = lax.broadcasted_iota(jnp.int32, own.shape, 1)
    lower = (lane // 16) % 2 == 1
    has_left = jnp.where(gx > 0, 0.25, 0.0)
    has_right = jnp.where(gx < gx_size - 1, 0.25, 0.0)
    swapped = jnp.where(lower, pltpu.roll(own, 16, 1), pltpu.roll(own, 128 - 16, 1))
    outside = jnp.where(
        lower,
        has_left * pltpu.roll(beside[0], 16, 1),
        has_right * pltpu.roll(beside[1], 128 - 16, 1),
    )
    mixed[...] = pltpu.roll(0.5 * own + 0.25 * swapped + outside, lax.rem(8 * gy + 8, 128), 1)

    def exchange(step):
        partner = lax.rem(gy + step, gy_size)
        return pltpu.make_async_remote_copy(
            src_ref=mixed.at[pl.ds(partner, 1)],
            dst_ref=gathered.at[pl.ds(gy, 1)],
            send_sem=all_send,
            recv_sem=all_recv,
            device_id=(gx, partner),
            device_id_type=MESH,
        )

    def send(step, carry):
        exchange(step).start()
        return carry

    lax.fori_loop(1, gy_size, send, 0)
    gathered[pl.ds(gy, 1), :] = mixed[pl.ds(gy, 1), :]
    everyone = pltpu.make_async_remote_copy(
        src_ref=mixed.at[pl.ds(0, gy_size - 1)],
        dst_ref=gathered.at[pl.ds(0, gy_size - 1)],
        send_sem=all_send,
        recv_sem=all_recv,
        device_id=(gx, above),
        device_id_type=MESH,
    )
    everyone.wait_recv()

    lane = lax.broadcasted_iota(jnp.int32, (8, 128), 1)
    halves = [jnp.zeros((8, 128), jnp.float32) for _ in range(2)]
    for source in range(gy_size):
        spread = jnp.broadcast_to(gathered[pl.ds(source, 1), :], (8, 128))
        for half in range(2):
            turned = pltpu.roll(spread, 64 * half, 1, stride=8, stride_axis=0)
            halves[half] = jnp.where(lane // 8 == source, turned, halves[half])
    whole = jnp.concatenate(halves, axis=0)
    lane = lax.broadcasted_iota(jnp.int32, (16, 128), 1)
    before = jnp.where(lane == 0, 0.0, pltpu.roll(whole, 1, 1))
    after = jnp.where(lane == 127, 0.0, pltpu.roll(whole, 127, 1))
    final[...] = 0.5 * whole + 0.25 * (before + after)
    for x in range(2):
        fraction = final[pl.ds(12 + 2 * x, 2), :]
        divisor = jnp.maximum(fraction, 1.0)
        for component in range(3):
            velocity_ref[component, x] = final[pl.ds(4 * component + 2 * x, 2), :] / divisor / velocity_scale
        magnitude_ref[x] = fraction / 64.0

    for copy in flags + first_x + first_y + second_x + second_y + [to_right, to_left]:
        copy.wait_send()
    everyone.wait_send()


def local(gx_size, gy_size, populations, fluid):
    padded = (NX + 2, NY + 2 * TOP, NZ)
    vmem, dma = pltpu.VMEM, pltpu.SemaphoreType.DMA
    f32 = jnp.float32
    velocity, magnitude = pl.pallas_call(
        functools.partial(kernel, gx_size, gy_size),
        out_shape=(
            jax.ShapeDtypeStruct((3, 2, 2, 128), f32),
            jax.ShapeDtypeStruct((2, 2, 128), f32),
        ),
        in_specs=[pl.BlockSpec(memory_space=pl.ANY)] * 2,
        out_specs=(pl.BlockSpec(memory_space=pltpu.VMEM),) * 2,
        scratch_shapes=[
            vmem((19, NX, NY, NZ), f32),
            vmem((19, *padded), f32),
            vmem((19, *padded), f32),
            vmem((3, *padded), jnp.int32),
            vmem((256, 128), f32),
            vmem((32, 128), f32),
            vmem((2, 256, 128), f32),
            vmem((16, 128), f32),
            vmem((2, 16, 128), f32),
            vmem((16, 128), f32),
            vmem((16, 128), f32),
            vmem((16, 128), f32),
            dma((8,)),
            dma,
            dma((8,)),
            dma((8,)),
            dma((2, 9)),
            dma((2, 9)),
            dma((2,)),
            dma((2,)),
            dma,
            dma,
        ],
        compiler_params=pltpu.CompilerParams(
            collective_id=0, has_side_effects=True, vmem_limit_bytes=40 * 1024 * 1024
        ),
    )(populations, fluid)
    return jnp.swapaxes(velocity, 2, 3), jnp.swapaxes(magnitude, 1, 2)


def solution(mesh):
    return jax.shard_map(
        functools.partial(local, mesh.shape["gx"], mesh.shape["gy"]),
        mesh=mesh,
        in_specs=(P(None, "gx", "gy", None), P("gx", "gy", None)),
        out_specs=(P(None, "gx", None, "gy"), P("gx", None, "gy")),
        check_vma=False,
    )
```

time: 162 us -> 37.7 us (0.23)
  the two profiles are of different devices: /device:TPU:7 before, /device:TPU:1 now
where the time goes in v1:
time: 37.7 us; the launch traced here: 37.6 us
  Pallas kernels  33.2 us (88%)
  local copies, waits for them, and re-layouts  3.77 us (10%)
  between operations  0.65 us (2%)
    pallas_call x1, Pallas kernels, local(): pl.pallas_call(functools.partial(kernel, gx_size, gy_size), out_shape=(ja...  33.2 us
    unnamed x6, local copies, waits for them, and re-layouts  3.77 us

profile of v1, /device:TPU:1, one launch (start us, length us, event | category | flops | bytes accessed | tf_op | source)
XLA Modules:
  0.0 37.6 jit_solution(6827418517605096966)
XLA Ops:
  0.6 0.0 copy-start
  0.6 1.7 %copy-done = f32[19,8,32,128]{3,2,1,0:T(8,128)S(1)} copy-done((f32[19,8,32,128]{3,2,1,0:T(8,128)S(1)}, f32[19,8,32,128]{3,2,1,0:T(8,128)}, u32[]{:S(2)}) %copy-start) | copy-done | bytes 2490392
  2.3 0.0 copy-start.1
  2.3 0.9 %copy-done.1 = s32[8,32,128]{2,1,0:T(8,128)S(1)} copy-done((s32[8,32,128]{2,1,0:T(8,128)S(1)}, s32[8,32,128]{2,1,0:T(8,128)}, u32[]{:S(2)}) %copy-start.1) | copy-done | bytes 131096
  3.2 33.2 %shard_map.41 = (f32[3,2,2,128]{3,2,1,0:T(2,128)S(1)}, f32[2,2,128]{2,1,0:T(2,128)S(1)}) custom-call(f32[19,8,32,128]{3,2,1,0:T(8,128)S(1)} %copy-done, s32[8,32,128]{2,1,0:T(8,128)S(1)} %copy-done.1), custom_call_target="tpu_custom_call" | custom-call | tf_op jit(solution)/shard_map/pallas_call | solution.py:427
  36.4 0.6 %copy.6 = f32[3,2,128,2]{2,3,1,0:T(2,128)} copy(f32[3,2,128,2]{2,3,1,0:T(2,128)S(1)} %bitcast.2) | data formatting | bytes 12288
  37.0 0.6 %copy.7 = f32[2,128,2]{1,2,0:T(2,128)} copy(f32[2,128,2]{1,2,0:T(2,128)S(1)} %bitcast.3) | data formatting | bytes 4096
Async XLA Ops:
  0.6 1.7 %copy-start = (f32[19,8,32,128]{3,2,1,0:T(8,128)S(1)}, f32[19,8,32,128]{3,2,1,0:T(8,128)}, u32[]{:S(2)}) copy-start(f32[19,8,32,128]{3,2,1,0:T(8,128)} %populations.1) | copy-start | bytes 7471108
  2.3 0.9 %copy-start.1 = (s32[8,32,128]{2,1,0:T(8,128)S(1)}, s32[8,32,128]{2,1,0:T(8,128)}, u32[]{:S(2)}) copy-start(s32[8,32,128]{2,1,0:T(8,128)} %fluid.1) | copy-start | bytes 393220

commit v2 on v1

v2 whole, which is shorter than its diff:
```python
import functools

import jax
import jax.numpy as jnp
from jax import lax
from jax.experimental import pallas as pl
from jax.experimental.pallas import tpu as pltpu
from jax.sharding import PartitionSpec as P

MESH = pl.DeviceIdType.MESH

VELOCITIES = (
    (0, 0, 0),
    (1, 0, 0),
    (-1, 0, 0),
    (0, 1, 0),
    (0, -1, 0),
    (0, 0, 1),
    (0, 0, -1),
    (1, 1, 0),
    (-1, -1, 0),
    (1, -1, 0),
    (-1, 1, 0),
    (1, 0, 1),
    (-1, 0, -1),
    (1, 0, -1),
    (-1, 0, 1),
    (0, 1, 1),
    (0, -1, -1),
    (0, 1, -1),
    (0, -1, 1),
)
OPPOSITE = (0, 2, 1, 4, 3, 6, 5, 8, 7, 10, 9, 12, 11, 14, 13, 16, 15, 18, 17)
ORDER = (9, 1, 11, 13, 7, 3, 15, 17, 10, 2, 14, 12, 8, 4, 18, 16, 0, 5, 6)
SLOT = tuple(ORDER.index(channel) for channel in range(19))
relax_rate = 1.0 / 0.6
velocity_scale = 0.002

NX, NY, NZ = 8, 32, 128
TOP = 8
LAST = TOP + NY - 1
TILES = NY // 8


def moments(f):
    s = [f[i] + f[i + 1] for i in range(1, 19, 2)]
    d = [f[i] - f[i + 1] for i in range(1, 19, 2)]
    rho = (f[0] + s[8]) + ((s[0] + s[1]) + (s[2] + s[3])) + ((s[4] + s[5]) + (s[6] + s[7]))
    mx = d[0] + (d[3] + d[4]) + (d[5] + d[6])
    my = d[1] + (d[3] - d[4]) + (d[7] + d[8])
    mz = d[2] + (d[5] - d[6]) + (d[7] - d[8])
    return rho, mx, my, mz


def collide(f):
    rho, mx, my, mz = moments(f)
    inverse = 1.0 / rho
    ux, uy, uz = mx * inverse, my * inverse, mz * inverse
    base = rho - 1.5 * (mx * ux + my * uy + mz * uz)
    keep = 1.0 - relax_rate
    relaxed = [keep * f[0] + (relax_rate / 3.0) * base]
    vx, vy, vz = 1.5 * ux, 1.5 * uy, 1.5 * uz
    near = (relax_rate / 18.0) * base
    far = (relax_rate / 36.0) * base
    ax, ay, az = (relax_rate / 6.0) * mx, (relax_rate / 6.0) * my, (relax_rate / 6.0) * mz
    bx, by, bz = 0.5 * ax, 0.5 * ay, 0.5 * az
    for channel, level, flow, speed in (
        (1, near, ax, vx),
        (3, near, ay, vy),
        (5, near, az, vz),
        (7, far, bx + by, vx + vy),
        (9, far, bx - by, vx - vy),
        (11, far, bx + bz, vx + vz),
        (13, far, bx - bz, vx - vz),
        (15, far, by + bz, vy + vz),
        (17, far, by - bz, vy - vz),
    ):
        even = level + flow * speed
        relaxed.append(keep * f[channel] + (even + flow))
        relaxed.append(keep * f[channel + 1] + (even - flow))
    return relaxed


def pulled(held, walls, x, tile):
    f = []
    for channel in range(19):
        cx, cy, cz = VELOCITIES[channel]
        rows = pl.ds(TOP + 8 * tile, 8)
        if channel == 0:
            f.append(held[SLOT[0], x + 1, rows, :])
            continue
        from_rows = pl.ds(TOP + 8 * tile - cy, 8)
        source = held[SLOT[channel], x + 1 - cx, from_rows, :]
        if cz:
            source = pltpu.roll(source, cz % NZ, 1)
        open_site = walls[cz % 3, x + 1 - cx, from_rows, :]
        f.append(jnp.where(open_site > 0, source, held[SLOT[OPPOSITE[channel]], x + 1, rows, :]))
    return f


def kernel(
    gx_size,
    gy_size,
    populations,
    fluid,
    velocity_ref,
    magnitude_ref,
    start,
    first,
    second,
    walls,
    sums,
    zmat,
    ymat,
    table,
    gathered,
    mixed,
    final,
    load_sem,
    fluid_sem,
    flag_send,
    flag_recv,
    halo_send,
    halo_recv,
    all_send,
    all_recv,
):
    gx, gy = lax.axis_index("gx"), lax.axis_index("gy")
    has_left, has_right = gx > 0, gx < gx_size - 1
    has_below, has_above = gy > 0, gy < gy_size - 1

    def load(x):
        return pltpu.make_async_copy(populations.at[:, x], start.at[:, x], load_sem.at[x])

    load(7).start()
    load(0).start()
    fluid_copy = pltpu.make_async_copy(fluid, walls.at[0, pl.ds(1, NX), pl.ds(TOP, NY), :], fluid_sem)
    fluid_copy.start()
    for x in range(1, NX - 1):
        load(x).start()

    barrier = pltpu.get_barrier_semaphore()

    def greet(x, begin):
        def one(step, carry):
            target = (x, lax.rem(gy + step, gy_size))
            pl.semaphore_signal(barrier, inc=1, device_id=target, device_id_type=MESH)
            return carry

        lax.fori_loop(begin, gy_size, one, 0)

    greet(gx, 1)
    pl.when(has_left)(lambda: greet(gx - 1, 0))
    pl.when(has_right)(lambda: greet(gx + 1, 0))

    def lane_walls(slab, rows):
        flags = walls[0, slab, rows, :]
        lane = lax.broadcasted_iota(jnp.int32, flags.shape, flags.ndim - 1)
        walls[1, slab, rows, :] = jnp.where(lane == 0, 0, pltpu.roll(flags, 1, flags.ndim - 1))
        walls[2, slab, rows, :] = jnp.where(lane == NZ - 1, 0, pltpu.roll(flags, NZ - 1, flags.ndim - 1))

    def wall_slab(slab, carry):
        for tile in range(TILES):
            lane_walls(slab, pl.ds(TOP + 8 * tile, 8))
        return carry

    def wall_rows(slab, carry):
        lane_walls(slab, low)
        lane_walls(slab, high)
        return carry

    inner, block = pl.ds(1, NX), pl.ds(TOP, NY)
    low, high = pl.ds(TOP - 1, 1), pl.ds(LAST + 1, 1)
    bottom, top = pl.ds(TOP, 1), pl.ds(LAST, 1)

    x_sides = [
        (pl.ds(0, 5), (NX, block), (0, block), (1, 0), has_right, has_left),
        (pl.ds(8, 5), (1, block), (NX + 1, block), (-1, 0), has_left, has_right),
        (pl.ds(4, 1), (NX, top), (0, low), (1, 1), has_right & has_above, has_left & has_below),
        (pl.ds(0, 1), (NX, bottom), (0, high), (1, -1), has_right & has_below, has_left & has_above),
        (pl.ds(8, 1), (1, top), (NX + 1, low), (-1, 1), has_left & has_above, has_right & has_below),
        (pl.ds(12, 1), (1, bottom), (NX + 1, high), (-1, -1), has_left & has_below, has_right & has_above),
    ]
    y_sides = [
        (pl.ds(4, 5), (inner, top), (inner, low), (0, 1), has_above, has_below),
        (pl.ds(12, 4), (inner, bottom), (inner, high), (0, -1), has_below, has_above),
        (pl.ds(0, 1), (inner, bottom), (inner, high), (0, -1), has_below, has_above),
    ]

    class Sides:
        def __init__(self, buffer, sides, slots, send, recv, offset):
            self.copies = [
                (
                    pltpu.make_async_remote_copy(
                        src_ref=buffer.at[(channels if slots else 0, *source)],
                        dst_ref=buffer.at[(channels if slots else 0, *target)],
                        send_sem=send.at[offset + i],
                        recv_sem=recv.at[offset + i],
                        device_id=(gx + way[0], gy + way[1]),
                        device_id_type=MESH,
                    ),
                    sent,
                    arrives,
                )
                for i, (channels, source, target, way, sent, arrives) in enumerate(sides)
            ]

        def start(self):
            for copy, sent, _ in self.copies:
                pl.when(sent)(copy.start)

        def wait_recv(self):
            for copy, _, arrives in self.copies:
                pl.when(arrives)(copy.wait_recv)

        def wait_send(self):
            for copy, sent, _ in self.copies:
                pl.when(sent)(copy.wait_send)

    flags = Sides(walls, x_sides + y_sides[:2], False, flag_send, flag_recv, 0)
    first_x = Sides(first, x_sides, True, halo_send.at[0], halo_recv.at[0], 0)
    first_y = Sides(first, y_sides, True, halo_send.at[0], halo_recv.at[0], 6)
    second_x = Sides(second, x_sides, True, halo_send.at[1], halo_recv.at[1], 0)
    second_y = Sides(second, y_sides, True, halo_send.at[1], halo_recv.at[1], 6)

    def relax_tile(x, tile):
        rows = pl.ds(8 * tile, 8)
        relaxed = collide([start[channel, x, rows, :] for channel in range(19)])
        for channel in range(19):
            first[SLOT[channel], x + 1, pl.ds(TOP + 8 * tile, 8), :] = relaxed[channel]

    def step_tile(x, tile):
        relaxed = collide(pulled(first, walls, x, tile))
        for channel in range(19):
            second[SLOT[channel], x + 1, pl.ds(TOP + 8 * tile, 8), :] = relaxed[channel]

    def sum_tile(x, tile):
        rho, mx, my, mz = moments(pulled(second, walls, x, tile))
        here = walls[0, x + 1, pl.ds(TOP + 8 * tile, 8), :].astype(jnp.float32)
        scale = here / rho
        for component, value in enumerate((mx * scale, my * scale, mz * scale, here)):
            rows = pl.ds(pl.multiple_of(component * 64 + (x // 4) * 32 + 8 * tile, 8), 8)
            sums[rows, :] = sums[rows, :] + value

    def over_slabs(body, edge, tiles):
        def edge_slab(step, carry):
            for tile in tiles:
                body((NX - 1) * (1 - step), tile)
            return carry

        def inner_slab(x, carry):
            for tile in tiles:
                body(x, tile)
            return carry

        if edge:
            lax.fori_loop(0, 2, edge_slab, 0)
        else:
            lax.fori_loop(1, NX - 1, inner_slab, 0)

    every, outer, middle = range(TILES), (0, TILES - 1), range(1, TILES - 1)

    load(7).wait()
    load(0).wait()
    over_slabs(relax_tile, True, every)
    columns = has_left.astype(jnp.int32) + has_right.astype(jnp.int32)
    pl.semaphore_wait(barrier, gy_size - 1 + gy_size * columns)
    first_x.start()
    fluid_copy.wait()
    flags.start()
    for x in range(1, NX - 1):
        load(x).wait()
    over_slabs(relax_tile, False, outer)
    first_y.start()
    over_slabs(relax_tile, False, middle)

    @pl.when(gx == 0)
    def _():
        walls[0, 0, pl.ds(TOP - 1, NY + 2), :] = jnp.zeros((NY + 2, NZ), jnp.int32)
        gathered[1] = jnp.zeros((16, 128), jnp.float32)

    @pl.when(gx == gx_size - 1)
    def _():
        walls[0, NX + 1, pl.ds(TOP - 1, NY + 2), :] = jnp.zeros((NY + 2, NZ), jnp.int32)
        gathered[2] = jnp.zeros((16, 128), jnp.float32)

    lax.fori_loop(1, NX + 1, wall_slab, 0)
    over_slabs(step_tile, False, middle)

    sums[...] = jnp.zeros(sums.shape, jnp.float32)
    row = lax.broadcasted_iota(jnp.int32, (32, NZ), 0)
    lane = lax.broadcasted_iota(jnp.int32, (32, NZ), 1)
    distance = jnp.abs(2 * (row & 15) + (row >> 4) - (lane >> 2))
    zmat[...] = jnp.where(distance == 0, 0.5, jnp.where(distance == 1, 0.25, 0.0)).astype(jnp.float32)

    def y_rows(step, carry):
        at = pl.multiple_of(8 * step, 8)
        row = lax.broadcasted_iota(jnp.int32, (8, 256), 0) + at
        column = lax.broadcasted_iota(jnp.int32, (8, 256), 1)
        hit = (((row >> 3) & 7) == 7 - (column >> 5)) & ((row & 7) == ((column >> 2) & 7))
        ymat[pl.ds(at, 8), :] = jnp.where(hit, 1.0, 0.0).astype(jnp.float32)
        return carry

    lax.fori_loop(0, 16, y_rows, 0)

    flags.wait_recv()

    @pl.when(gy == 0)
    def _():
        walls[0, :, low, :] = jnp.zeros((NX + 2, 1, NZ), jnp.int32)

    @pl.when(gy == gy_size - 1)
    def _():
        walls[0, :, high, :] = jnp.zeros((NX + 2, 1, NZ), jnp.int32)

    for slab in (0, NX + 1):
        wall_slab(slab, 0)
    lax.fori_loop(0, NX + 2, wall_rows, 0)

    first_y.wait_recv()
    over_slabs(step_tile, False, outer)
    first_x.wait_recv()
    over_slabs(step_tile, True, every)
    second_x.start()
    second_y.start()

    over_slabs(sum_tile, False, middle)
    second_y.wait_recv()
    over_slabs(sum_tile, False, outer)
    second_x.wait_recv()
    over_slabs(sum_tile, True, every)

    exact = dict(preferred_element_type=jnp.float32, precision=lax.Precision.HIGHEST)
    over_y = jnp.dot(ymat[...], sums[...], **exact)
    over_z = lax.dot_general(zmat[...], over_y, (((1,), (1,)), ((), ())), **exact)
    lane = lax.broadcasted_iota(jnp.int32, (16, 128), 1)
    table[...] = jnp.where(lane >= 64, over_z[:16], over_z[16:])

    def exchange(place, x, partner):
        return pltpu.make_async_remote_copy(
            src_ref=table.at[pl.ds(partner, 1)],
            dst_ref=gathered.at[place, pl.ds(gy, 1)],
            send_sem=all_send.at[place],
            recv_sem=all_recv.at[place],
            device_id=(x, partner),
            device_id_type=MESH,
        )

    def send(place, x, begin, end):
        def one(step, carry):
            exchange(place, x, lax.rem(gy + step, gy_size)).start()
            return carry

        lax.fori_loop(begin, end, one, 0)

    far = (gy_size // 2 - 3, gy_size // 2 + 4)
    send(0, gx, *far)
    pl.when(has_left)(lambda: send(2, gx - 1, *far))
    pl.when(has_right)(lambda: send(1, gx + 1, *far))
    send(0, gx, far[1], gy_size)
    send(0, gx, 1, far[0])
    pl.when(has_left)(lambda: send(2, gx - 1, far[1], gy_size + far[0]))
    pl.when(has_right)(lambda: send(1, gx + 1, far[1], gy_size + far[0]))
    gathered[0, pl.ds(gy, 1), :] = table[pl.ds(gy, 1), :]

    def everyone(place, count):
        return pltpu.make_async_remote_copy(
            src_ref=table.at[pl.ds(0, count)],
            dst_ref=gathered.at[place, pl.ds(0, count)],
            send_sem=all_send.at[place],
            recv_sem=all_recv.at[place],
            device_id=(gx, lax.rem(gy + 1, gy_size)),
            device_id_type=MESH,
        )

    column, from_left, from_right = everyone(0, gy_size - 1), everyone(1, gy_size), everyone(2, gy_size)
    column.wait_recv()
    pl.when(has_left)(from_left.wait_recv)
    pl.when(has_right)(from_right.wait_recv)

    lower = (lane & 8) != 0
    own = gathered[0]
    beside = jnp.where(
        lower,
        pltpu.roll(own, 8, 1) + pltpu.roll(gathered[1], 8, 1),
        pltpu.roll(own, 120, 1) + pltpu.roll(gathered[2], 120, 1),
    )
    along_x = pltpu.roll(0.5 * own + 0.25 * beside, 8, 1)

    mixed[pl.ds(0, 8), :] = pltpu.roll(along_x[:8], 0, 1, stride=8, stride_axis=0)
    mixed[pl.ds(8, 8), :] = pltpu.roll(along_x[8:], 64, 1, stride=8, stride_axis=0)
    lane = lax.broadcasted_iota(jnp.int32, (8, 128), 1)
    halves = [jnp.zeros((8, 128), jnp.float32) for _ in range(2)]
    for source in range(gy_size):
        spread = jnp.broadcast_to(mixed[pl.ds(source, 1), :], (8, 128))
        for half in range(2):
            turned = pltpu.roll(spread, 64 * half, 1, stride=8, stride_axis=0)
            halves[half] = jnp.where(lane >> 3 == source, turned, halves[half])
    for half in range(2):
        whole = halves[half]
        before = jnp.where(lane == 0, 0.0, pltpu.roll(whole, 1, 1))
        after = jnp.where(lane == 127, 0.0, pltpu.roll(whole, 127, 1))
        final[pl.ds(8 * half, 8), :] = 0.5 * whole + 0.25 * (before + after)
    for x in range(2):
        for z in range(2):
            fraction = final[pl.ds(8 * z + 6 + x, 1), :]
            divisor = jnp.maximum(fraction, 1.0)
            for component in range(3):
                voxels = final[pl.ds(8 * z + 2 * component + x, 1), :]
                velocity_ref[component, x, pl.ds(z, 1), :] = voxels / divisor / velocity_scale
            magnitude_ref[x, pl.ds(z, 1), :] = fraction / 64.0

    for sides in (flags, first_x, first_y, second_x, second_y):
        sides.wait_send()
    column.wait_send()
    pl.when(has_left)(from_right.wait_send)
    pl.when(has_right)(from_left.wait_send)


def local(gx_size, gy_size, populations, fluid):
    padded = (NX + 2, NY + 2 * TOP, NZ)
    vmem, dma = pltpu.VMEM, pltpu.SemaphoreType.DMA
    f32 = jnp.float32
    velocity, magnitude = pl.pallas_call(
        functools.partial(kernel, gx_size, gy_size),
        out_shape=(
            jax.ShapeDtypeStruct((3, 2, 2, 128), f32),
            jax.ShapeDtypeStruct((2, 2, 128), f32),
        ),
        in_specs=[pl.BlockSpec(memory_space=pltpu.HBM)] * 2,
        out_specs=(pl.BlockSpec(memory_space=pltpu.VMEM),) * 2,
        scratch_shapes=[
            vmem((19, NX, NY, NZ), f32),
            vmem((19, *padded), f32),
            vmem((19, *padded), f32),
            vmem((3, *padded), jnp.int32),
            vmem((256, 128), f32),
            vmem((32, 128), f32),
            vmem((128, 256), f32),
            vmem((16, 128), f32),
            vmem((3, 16, 128), f32),
            vmem((16, 128), f32),
            vmem((16, 128), f32),
            dma((8,)),
            dma,
            dma((8,)),
            dma((8,)),
            dma((2, 9)),
            dma((2, 9)),
            dma((3,)),
            dma((3,)),
        ],
        compiler_params=pltpu.CompilerParams(
            collective_id=0, has_side_effects=True, vmem_limit_bytes=58 * 1024 * 1024
        ),
    )(populations, fluid)
    return jnp.swapaxes(velocity, 2, 3), jnp.swapaxes(magnitude, 1, 2)


def solution(mesh):
    return jax.shard_map(
        functools.partial(local, mesh.shape["gx"], mesh.shape["gy"]),
        mesh=mesh,
        in_specs=(P(None, "gx", "gy", None), P("gx", "gy", None)),
        out_specs=(P(None, "gx", None, "gy"), P("gx", None, "gy")),
        check_vma=False,
    )
```

time: 37.7 us -> 33.2 us (0.88)
  the two profiles are of different devices: /device:TPU:1 before, /device:TPU:7 now
where the time goes in v2:
time: 33.2 us; the launch traced here: 33 us
  Pallas kernels  29.9 us (90%)
  local copies, waits for them, and re-layouts  2.52 us (8%)
  between operations  0.64 us (2%)
    pallas_call x1, Pallas kernels, local(): pl.pallas_call(functools.partial(kernel, gx_size, gy_size), out_shape=(ja...  29.9 us
    unnamed x2, local copies, waits for them, and re-layouts  2.52 us

profile of v2, /device:TPU:7, one launch (start us, length us, event | category | flops | bytes accessed | tf_op | source)
XLA Modules:
  0.0 33.0 jit_solution(17608294541584183269)
XLA Ops:
  0.6 29.9 %shard_map.41 = (f32[3,2,2,128]{3,2,1,0:T(2,128)}, f32[2,2,128]{2,1,0:T(2,128)}) custom-call(f32[19,8,32,128]{3,2,1,0:T(8,128)} %populations.1, s32[8,32,128]{2,1,0:T(8,128)} %fluid.1), custom_call_target="tpu_custom_call" | custom-call | tf_op jit(solution)/shard_map/pallas_call | solution.py:424
  30.5 1.3 %copy.6 = f32[3,2,128,2]{2,3,1,0:T(2,128)} copy(f32[3,2,128,2]{2,3,1,0:T(2,128)} %bitcast.2) | data formatting | bytes 12288
  31.8 1.2 %copy.7 = f32[2,128,2]{1,2,0:T(2,128)} copy(f32[2,128,2]{1,2,0:T(2,128)} %bitcast.3) | data formatting | bytes 4096

commit v3 on v2

--- a/solution.py
+++ b/solution.py
@@ -116,6 +116,7 @@
     gathered,
     mixed,
     final,
+    ready,
     load_sem,
     fluid_sem,
     flag_send,
@@ -132,26 +133,38 @@
     def load(x):
         return pltpu.make_async_copy(populations.at[:, x], start.at[:, x], load_sem.at[x])
 
+    fluid_copy = pltpu.make_async_copy(fluid, walls.at[0, pl.ds(1, NX), pl.ds(TOP, NY), :], fluid_sem)
     load(7).start()
     load(0).start()
-    fluid_copy = pltpu.make_async_copy(fluid, walls.at[0, pl.ds(1, NX), pl.ds(TOP, NY), :], fluid_sem)
     fluid_copy.start()
     for x in range(1, NX - 1):
         load(x).start()
 
+    def number(*conditions):
+        return sum(condition.astype(jnp.int32) for condition in conditions)
+
     barrier = pltpu.get_barrier_semaphore()
-
-    def greet(x, begin):
-        def one(step, carry):
-            target = (x, lax.rem(gy + step, gy_size))
-            pl.semaphore_signal(barrier, inc=1, device_id=target, device_id_type=MESH)
-            return carry
-
-        lax.fori_loop(begin, gy_size, one, 0)
-
-    greet(gx, 1)
-    pl.when(has_left)(lambda: greet(gx - 1, 0))
-    pl.when(has_right)(lambda: greet(gx + 1, 0))
+    beside_x = ((-1, has_left), (0, None), (1, has_right))
+    beside_y = ((-1, has_below), (0, None), (1, has_above))
+    for dx, in_x in beside_x:
+        for dy, in_y in beside_y:
+            if dx == 0 and dy == 0:
+                continue
+            there = in_y if in_x is None else in_x if in_y is None else in_x & in_y
+
+            @pl.when(there)
+            def _():
+                pl.semaphore_signal(barrier, inc=1, device_id=(gx + dx, gy + dy), device_id_type=MESH)
+
+    def tell(stage):
+        for way in (-(2**stage), 2**stage):
+
+            @pl.when((gy + way >= 0) & (gy + way < gy_size))
+            def _():
+                pl.semaphore_signal(ready.at[stage], inc=1, device_id=(gx, gy + way), device_id_type=MESH)
+
+    def hear(stage):
+        pl.semaphore_wait(ready.at[stage], number(gy >= 2**stage, gy + 2**stage < gy_size))
 
     def lane_walls(slab, rows):
         flags = walls[0, slab, rows, :]
@@ -162,11 +175,6 @@
     def wall_slab(slab, carry):
         for tile in range(TILES):
             lane_walls(slab, pl.ds(TOP + 8 * tile, 8))
-        return carry
-
-    def wall_rows(slab, carry):
-        lane_walls(slab, low)
-        lane_walls(slab, high)
         return carry
 
     inner, block = pl.ds(1, NX), pl.ds(TOP, NY)
@@ -205,8 +213,8 @@
                 for i, (channels, source, target, way, sent, arrives) in enumerate(sides)
             ]
 
-        def start(self):
-            for copy, sent, _ in self.copies:
+        def start(self, begin=0, end=None):
+            for copy, sent, _ in self.copies[begin:end]:
                 pl.when(sent)(copy.start)
 
         def wait_recv(self):
@@ -263,16 +271,20 @@
     load(7).wait()
     load(0).wait()
     over_slabs(relax_tile, True, every)
-    columns = has_left.astype(jnp.int32) + has_right.astype(jnp.int32)
-    pl.semaphore_wait(barrier, gy_size - 1 + gy_size * columns)
-    first_x.start()
     fluid_copy.wait()
-    flags.start()
+    pl.semaphore_wait(barrier, (1 + number(has_left, has_right)) * (1 + number(has_below, has_above)) - 1)
+    flags.start(0, 2)
+    first_x.start(0, 2)
+    flags.start(2)
+    first_x.start(2)
+    tell(0)
     for x in range(1, NX - 1):
         load(x).wait()
     over_slabs(relax_tile, False, outer)
     first_y.start()
     over_slabs(relax_tile, False, middle)
+    hear(0)
+    tell(1)
 
     @pl.when(gx == 0)
     def _():
@@ -286,6 +298,8 @@
 
     lax.fori_loop(1, NX + 1, wall_slab, 0)
     over_slabs(step_tile, False, middle)
+    hear(1)
+    tell(2)
 
     sums[...] = jnp.zeros(sums.shape, jnp.float32)
     row = lax.broadcasted_iota(jnp.int32, (32, NZ), 0)
@@ -315,7 +329,8 @@
 
     for slab in (0, NX + 1):
         wall_slab(slab, 0)
-    lax.fori_loop(0, NX + 2, wall_rows, 0)
+    for row in (TOP - 1, LAST + 1):
+        lane_walls(inner, row)
 
     first_y.wait_recv()
     over_slabs(step_tile, False, outer)
@@ -323,6 +338,8 @@
     over_slabs(step_tile, True, every)
     second_x.start()
     second_y.start()
+    hear(2)
+    tell(3)
 
     over_slabs(sum_tile, False, middle)
     second_y.wait_recv()
@@ -330,11 +347,21 @@
     second_x.wait_recv()
     over_slabs(sum_tile, True, every)
 
-    exact = dict(preferred_element_type=jnp.float32, precision=lax.Precision.HIGHEST)
-    over_y = jnp.dot(ymat[...], sums[...], **exact)
-    over_z = lax.dot_general(zmat[...], over_y, (((1,), (1,)), ((), ())), **exact)
+    def parts(value):
+        upper = value.astype(jnp.bfloat16)
+        return upper, (value - upper.astype(jnp.float32)).astype(jnp.bfloat16)
+
+    weights = ymat[...].astype(jnp.bfloat16)
+    over_y = sum(jnp.dot(weights, part, preferred_element_type=jnp.float32) for part in parts(sums[...]))
+    weights = zmat[...].astype(jnp.bfloat16)
+    over_z = sum(
+        lax.dot_general(weights, part, (((1,), (1,)), ((), ())), preferred_element_type=jnp.float32)
+        for part in parts(over_y)
+    )
     lane = lax.broadcasted_iota(jnp.int32, (16, 128), 1)
     table[...] = jnp.where(lane >= 64, over_z[:16], over_z[16:])
+
+    hear(3)
 
     def exchange(place, x, partner):
         return pltpu.make_async_remote_copy(
@@ -441,6 +468,7 @@
             vmem((3, 16, 128), f32),
             vmem((16, 128), f32),
             vmem((16, 128), f32),
+            pltpu.SemaphoreType.REGULAR((4,)),
             dma((8,)),
             dma,
             dma((8,)),
@@ -451,7 +479,7 @@
             dma((3,)),
         ],
         compiler_params=pltpu.CompilerParams(
-            collective_id=0, has_side_effects=True, vmem_limit_bytes=58 * 1024 * 1024
+            collective_id=0, has_side_effects=True, vmem_limit_bytes=55200 * 1024
         ),
     )(populations, fluid)
     return jnp.swapaxes(velocity, 2, 3), jnp.swapaxes(magnitude, 1, 2)

time: 33.2 us -> 27.9 us (0.84)
  Pallas kernels: 29.9 us -> 25.9 us
  local copies, waits for them, and re-layouts: 2.52 us -> 1.17 us
    pallas_call x1, Pallas kernels: 29.9 us -> 25.9 us  [local(): pl.pallas_call(functools.partial(kernel, gx_size, gy_size), out_shape=(ja...]
    unnamed x2, local copies, waits for them, and re-layouts: 2.52 us -> 1.17 us
where the time goes in v3:
time: 27.9 us; the launch traced here: 27.8 us
  Pallas kernels  25.9 us (93%)
  local copies, waits for them, and re-layouts  1.17 us (4%)
  between operations  0.64 us (2%)
    pallas_call x1, Pallas kernels, local(): pl.pallas_call(functools.partial(kernel, gx_size, gy_size), out_shape=(ja...  25.9 us
    unnamed x2, local copies, waits for them, and re-layouts  1.17 us

profile of v3, /device:TPU:7, one launch (start us, length us, event | category | flops | bytes accessed | tf_op | source)
XLA Modules:
  0.0 27.8 jit_solution(6634425790943141708)
XLA Ops:
  0.6 25.9 %shard_map.41 = (f32[3,2,2,128]{3,2,1,0:T(2,128)S(1)}, f32[2,2,128]{2,1,0:T(2,128)S(1)}) custom-call(f32[19,8,32,128]{3,2,1,0:T(8,128)} %populations.1, s32[8,32,128]{2,1,0:T(8,128)} %fluid.1), custom_call_target="tpu_custom_call" | custom-call | tf_op jit(solution)/shard_map/pallas_call | solution.py:451
  26.6 0.6 %copy.6 = f32[3,2,128,2]{2,3,1,0:T(2,128)} copy(f32[3,2,128,2]{2,3,1,0:T(2,128)S(1)} %bitcast.2) | data formatting | bytes 12288
  27.2 0.6 %copy.7 = f32[2,128,2]{1,2,0:T(2,128)} copy(f32[2,128,2]{1,2,0:T(2,128)S(1)} %bitcast.3) | data formatting | bytes 4096

commit v4 on v3

--- a/solution.py
+++ b/solution.py
@@ -31,7 +31,8 @@
     (0, -1, 1),
 )
 OPPOSITE = (0, 2, 1, 4, 3, 6, 5, 8, 7, 10, 9, 12, 11, 14, 13, 16, 15, 18, 17)
-ORDER = (9, 1, 11, 13, 7, 3, 15, 17, 10, 2, 14, 12, 8, 4, 18, 16, 0, 5, 6)
+FLAG = -1
+ORDER = (FLAG, 9, 1, 11, 13, 7, FLAG, 3, 15, 17, FLAG, 10, 2, 14, 12, 8, FLAG, 4, 18, 16, 0, 5, 6)
 SLOT = tuple(ORDER.index(channel) for channel in range(19))
 relax_rate = 1.0 / 0.6
 velocity_scale = 0.002
@@ -103,9 +104,9 @@
     gy_size,
     populations,
     fluid,
-    velocity_ref,
-    magnitude_ref,
+    final,
     start,
+    solid,
     first,
     second,
     walls,
@@ -115,25 +116,23 @@
     table,
     gathered,
     mixed,
-    final,
     ready,
     load_sem,
     fluid_sem,
-    flag_send,
-    flag_recv,
     halo_send,
     halo_recv,
     all_send,
     all_recv,
 ):
     gx, gy = lax.axis_index("gx"), lax.axis_index("gy")
+    f32 = jnp.float32
     has_left, has_right = gx > 0, gx < gx_size - 1
     has_below, has_above = gy > 0, gy < gy_size - 1
 
     def load(x):
         return pltpu.make_async_copy(populations.at[:, x], start.at[:, x], load_sem.at[x])
 
-    fluid_copy = pltpu.make_async_copy(fluid, walls.at[0, pl.ds(1, NX), pl.ds(TOP, NY), :], fluid_sem)
+    fluid_copy = pltpu.make_async_copy(fluid, solid, fluid_sem)
     load(7).start()
     load(0).start()
     fluid_copy.start()
@@ -169,39 +168,53 @@
     def lane_walls(slab, rows):
         flags = walls[0, slab, rows, :]
         lane = lax.broadcasted_iota(jnp.int32, flags.shape, flags.ndim - 1)
-        walls[1, slab, rows, :] = jnp.where(lane == 0, 0, pltpu.roll(flags, 1, flags.ndim - 1))
-        walls[2, slab, rows, :] = jnp.where(lane == NZ - 1, 0, pltpu.roll(flags, NZ - 1, flags.ndim - 1))
-
-    def wall_slab(slab, carry):
+        walls[1, slab, rows, :] = jnp.where(lane == 0, 0.0, pltpu.roll(flags, 1, flags.ndim - 1))
+        walls[2, slab, rows, :] = jnp.where(lane == NZ - 1, 0.0, pltpu.roll(flags, NZ - 1, flags.ndim - 1))
+
+    def inner_walls(x, carry):
         for tile in range(TILES):
-            lane_walls(slab, pl.ds(TOP + 8 * tile, 8))
+            rows = pl.ds(TOP + 8 * tile, 8)
+            walls[0, x + 1, rows, :] = solid[x, pl.ds(8 * tile, 8), :].astype(jnp.float32)
+            lane_walls(x + 1, rows)
+        return carry
+
+    def face_flags(x, carry):
+        upper = solid[x, pl.ds(NY - 8, 8), :].astype(jnp.float32)
+        lower = solid[x, pl.ds(0, 8), :].astype(jnp.float32)
+        for slot in (6, 10):
+            first[slot, x + 1, pl.ds(TOP + NY - 8, 8), :] = upper
+            second[slot, x + 1, pl.ds(TOP + NY - 8, 8), :] = upper
+        first[16, x + 1, pl.ds(TOP, 8), :] = lower
+        second[16, x + 1, pl.ds(TOP, 8), :] = lower
         return carry
 
     inner, block = pl.ds(1, NX), pl.ds(TOP, NY)
     low, high = pl.ds(TOP - 1, 1), pl.ds(LAST + 1, 1)
     bottom, top = pl.ds(TOP, 1), pl.ds(LAST, 1)
 
-    x_sides = [
-        (pl.ds(0, 5), (NX, block), (0, block), (1, 0), has_right, has_left),
-        (pl.ds(8, 5), (1, block), (NX + 1, block), (-1, 0), has_left, has_right),
-        (pl.ds(4, 1), (NX, top), (0, low), (1, 1), has_right & has_above, has_left & has_below),
-        (pl.ds(0, 1), (NX, bottom), (0, high), (1, -1), has_right & has_below, has_left & has_above),
-        (pl.ds(8, 1), (1, top), (NX + 1, low), (-1, 1), has_left & has_above, has_right & has_below),
-        (pl.ds(12, 1), (1, bottom), (NX + 1, high), (-1, -1), has_left & has_below, has_right & has_above),
+    def x_sides(flags):
+        return [
+            (pl.ds(5, 1 + flags), (NX, top), (0, low), (1, 1), has_right & has_above, has_left & has_below),
+            (pl.ds(1 - flags, 1 + flags), (NX, bottom), (0, high), (1, -1), has_right & has_below, has_left & has_above),
+            (pl.ds(11 - flags, 1 + flags), (1, top), (NX + 1, low), (-1, 1), has_left & has_above, has_right & has_below),
+            (pl.ds(15, 1 + flags), (1, bottom), (NX + 1, high), (-1, -1), has_left & has_below, has_right & has_above),
+            (pl.ds(1, 5 + flags), (NX, block), (0, block), (1, 0), has_right, has_left),
+            (pl.ds(11, 5 + flags), (1, block), (NX + 1, block), (-1, 0), has_left, has_right),
+        ]
+
+    y_sides = [
+        (pl.ds(5, 7), (inner, top), (inner, low), (0, 1), has_above, has_below),
+        (pl.ds(15, 5), (inner, bottom), (inner, high), (0, -1), has_below, has_above),
+        (pl.ds(1, 1), (inner, bottom), (inner, high), (0, -1), has_below, has_above),
     ]
-    y_sides = [
-        (pl.ds(4, 5), (inner, top), (inner, low), (0, 1), has_above, has_below),
-        (pl.ds(12, 4), (inner, bottom), (inner, high), (0, -1), has_below, has_above),
-        (pl.ds(0, 1), (inner, bottom), (inner, high), (0, -1), has_below, has_above),
-    ]
 
     class Sides:
-        def __init__(self, buffer, sides, slots, send, recv, offset):
+        def __init__(self, buffer, sides, send, recv, offset):
             self.copies = [
                 (
                     pltpu.make_async_remote_copy(
-                        src_ref=buffer.at[(channels if slots else 0, *source)],
-                        dst_ref=buffer.at[(channels if slots else 0, *target)],
+                        src_ref=buffer.at[(channels, *source)],
+                        dst_ref=buffer.at[(channels, *target)],
                         send_sem=send.at[offset + i],
                         recv_sem=recv.at[offset + i],
                         device_id=(gx + way[0], gy + way[1]),
@@ -213,8 +226,8 @@
                 for i, (channels, source, target, way, sent, arrives) in enumerate(sides)
             ]
 
-        def start(self, begin=0, end=None):
-            for copy, sent, _ in self.copies[begin:end]:
+        def start(self):
+            for copy, sent, _ in self.copies:
                 pl.when(sent)(copy.start)
 
         def wait_recv(self):
@@ -225,11 +238,10 @@
             for copy, sent, _ in self.copies:
                 pl.when(sent)(copy.wait_send)
 
-    flags = Sides(walls, x_sides + y_sides[:2], False, flag_send, flag_recv, 0)
-    first_x = Sides(first, x_sides, True, halo_send.at[0], halo_recv.at[0], 0)
-    first_y = Sides(first, y_sides, True, halo_send.at[0], halo_recv.at[0], 6)
-    second_x = Sides(second, x_sides, True, halo_send.at[1], halo_recv.at[1], 0)
-    second_y = Sides(second, y_sides, True, halo_send.at[1], halo_recv.at[1], 6)
+    first_x = Sides(first, x_sides(1), halo_send.at[0], halo_recv.at[0], 0)
+    first_y = Sides(first, y_sides, halo_send.at[0], halo_recv.at[0], 6)
+    second_x = Sides(second, x_sides(0), halo_send.at[1], halo_recv.at[1], 0)
+    second_y = Sides(second, y_sides, halo_send.at[1], halo_recv.at[1], 6)
 
     def relax_tile(x, tile):
         rows = pl.ds(8 * tile, 8)
@@ -244,7 +256,7 @@
 
     def sum_tile(x, tile):
         rho, mx, my, mz = moments(pulled(second, walls, x, tile))
-        here = walls[0, x + 1, pl.ds(TOP + 8 * tile, 8), :].astype(jnp.float32)
+        here = walls[0, x + 1, pl.ds(TOP + 8 * tile, 8), :]
         scale = here / rho
         for component, value in enumerate((mx * scale, my * scale, mz * scale, here)):
             rows = pl.ds(pl.multiple_of(component * 64 + (x // 4) * 32 + 8 * tile, 8), 8)
@@ -267,39 +279,6 @@
             lax.fori_loop(1, NX - 1, inner_slab, 0)
 
     every, outer, middle = range(TILES), (0, TILES - 1), range(1, TILES - 1)
-
-    load(7).wait()
-    load(0).wait()
-    over_slabs(relax_tile, True, every)
-    fluid_copy.wait()
-    pl.semaphore_wait(barrier, (1 + number(has_left, has_right)) * (1 + number(has_below, has_above)) - 1)
-    flags.start(0, 2)
-    first_x.start(0, 2)
-    flags.start(2)
-    first_x.start(2)
-    tell(0)
-    for x in range(1, NX - 1):
-        load(x).wait()
-    over_slabs(relax_tile, False, outer)
-    first_y.start()
-    over_slabs(relax_tile, False, middle)
-    hear(0)
-    tell(1)
-
-    @pl.when(gx == 0)
-    def _():
-        walls[0, 0, pl.ds(TOP - 1, NY + 2), :] = jnp.zeros((NY + 2, NZ), jnp.int32)
-        gathered[1] = jnp.zeros((16, 128), jnp.float32)
-
-    @pl.when(gx == gx_size - 1)
-    def _():
-        walls[0, NX + 1, pl.ds(TOP - 1, NY + 2), :] = jnp.zeros((NY + 2, NZ), jnp.int32)
-        gathered[2] = jnp.zeros((16, 128), jnp.float32)
-
-    lax.fori_loop(1, NX + 1, wall_slab, 0)
-    over_slabs(step_tile, False, middle)
-    hear(1)
-    tell(2)
 
     sums[...] = jnp.zeros(sums.shape, jnp.float32)
     row = lax.broadcasted_iota(jnp.int32, (32, NZ), 0)
@@ -317,24 +296,71 @@
 
     lax.fori_loop(0, 16, y_rows, 0)
 
-    flags.wait_recv()
+    @pl.when(gx == 0)
+    def _():
+        first[6, 0, pl.ds(TOP, NY), :] = jnp.zeros((NY, NZ), f32)
+        first[6, 0, low, :] = jnp.zeros((1, NZ), f32)
+        first[0, 0, high, :] = jnp.zeros((1, NZ), f32)
+        gathered[1] = jnp.zeros((16, 128), f32)
+
+    @pl.when(gx == gx_size - 1)
+    def _():
+        first[16, NX + 1, pl.ds(TOP, NY), :] = jnp.zeros((NY, NZ), f32)
+        first[10, NX + 1, low, :] = jnp.zeros((1, NZ), f32)
+        first[16, NX + 1, high, :] = jnp.zeros((1, NZ), f32)
+        gathered[2] = jnp.zeros((16, 128), f32)
 
     @pl.when(gy == 0)
     def _():
-        walls[0, :, low, :] = jnp.zeros((NX + 2, 1, NZ), jnp.int32)
+        first[6, inner, TOP - 1, :] = jnp.zeros((NX, NZ), f32)
+        first[6, 0, low, :] = jnp.zeros((1, NZ), f32)
+        first[10, NX + 1, low, :] = jnp.zeros((1, NZ), f32)
 
     @pl.when(gy == gy_size - 1)
     def _():
-        walls[0, :, high, :] = jnp.zeros((NX + 2, 1, NZ), jnp.int32)
-
-    for slab in (0, NX + 1):
-        wall_slab(slab, 0)
-    for row in (TOP - 1, LAST + 1):
+        first[16, inner, LAST + 1, :] = jnp.zeros((NX, NZ), f32)
+        first[0, 0, high, :] = jnp.zeros((1, NZ), f32)
+        first[16, NX + 1, high, :] = jnp.zeros((1, NZ), f32)
+
+    load(7).wait()
+    load(0).wait()
+    over_slabs(relax_tile, True, every)
+    fluid_copy.wait()
+    lax.fori_loop(0, NX, face_flags, 0)
+    for tile in range(TILES):
+        rows, own = pl.ds(TOP + 8 * tile, 8), pl.ds(8 * tile, 8)
+        first[6, NX, rows, :] = solid[NX - 1, own, :].astype(f32)
+        first[16, 1, rows, :] = solid[0, own, :].astype(f32)
+    first[0, NX, pl.ds(TOP, 8), :] = solid[NX - 1, pl.ds(0, 8), :].astype(f32)
+    for x in range(1, NX - 1):
+        load(x).wait()
+    over_slabs(relax_tile, False, outer)
+    over_slabs(relax_tile, False, middle)
+    pl.semaphore_wait(barrier, (1 + number(has_left, has_right)) * (1 + number(has_below, has_above)) - 1)
+    first_x.start()
+    first_y.start()
+    tell(0)
+
+    lax.fori_loop(0, NX, inner_walls, 0)
+    over_slabs(step_tile, False, middle)
+    hear(0)
+    tell(1)
+
+    first_y.wait_recv()
+    for slot, row in ((6, TOP - 1), (16, LAST + 1)):
+        walls[0, inner, row, :] = first[slot, inner, row, :]
         lane_walls(inner, row)
-
-    first_y.wait_recv()
     over_slabs(step_tile, False, outer)
+    hear(1)
+    tell(2)
     first_x.wait_recv()
+    for slot, slab in ((6, 0), (16, NX + 1)):
+        for tile in range(TILES):
+            rows = pl.ds(TOP + 8 * tile, 8)
+            walls[0, slab, rows, :] = first[slot, slab, rows, :]
+            lane_walls(slab, rows)
+    for slot, slab, row in ((6, 0, low), (0, 0, high), (10, NX + 1, low), (16, NX + 1, high)):
+        walls[0, slab, row, :] = first[slot, slab, row, :]
     over_slabs(step_tile, True, every)
     second_x.start()
     second_y.start()
@@ -342,6 +368,8 @@
     tell(3)
 
     over_slabs(sum_tile, False, middle)
+    for sides in (first_x, first_y):
+        sides.wait_send()
     second_y.wait_recv()
     over_slabs(sum_tile, False, outer)
     second_x.wait_recv()
@@ -374,11 +402,8 @@
         )
 
     def send(place, x, begin, end):
-        def one(step, carry):
+        for step in range(begin, end):
             exchange(place, x, lax.rem(gy + step, gy_size)).start()
-            return carry
-
-        lax.fori_loop(begin, end, one, 0)
 
     far = (gy_size // 2 - 3, gy_size // 2 + 4)
     send(0, gx, *far)
@@ -401,6 +426,11 @@
         )
 
     column, from_left, from_right = everyone(0, gy_size - 1), everyone(1, gy_size), everyone(2, gy_size)
+    second_x.wait_send()
+    second_y.wait_send()
+    column.wait_send()
+    pl.when(has_left)(from_right.wait_send)
+    pl.when(has_right)(from_left.wait_send)
     column.wait_recv()
     pl.when(has_left)(from_left.wait_recv)
     pl.when(has_right)(from_right.wait_recv)
@@ -428,6 +458,9 @@
         before = jnp.where(lane == 0, 0.0, pltpu.roll(whole, 1, 1))
         after = jnp.where(lane == 127, 0.0, pltpu.roll(whole, 127, 1))
         final[pl.ds(8 * half, 8), :] = 0.5 * whole + 0.25 * (before + after)
+
+
+def finish(final, velocity_ref, magnitude_ref):
     for x in range(2):
         for z in range(2):
             fraction = final[pl.ds(8 * z + 6 + x, 1), :]
@@ -437,42 +470,31 @@
                 velocity_ref[component, x, pl.ds(z, 1), :] = voxels / divisor / velocity_scale
             magnitude_ref[x, pl.ds(z, 1), :] = fraction / 64.0
 
-    for sides in (flags, first_x, first_y, second_x, second_y):
-        sides.wait_send()
-    column.wait_send()
-    pl.when(has_left)(from_right.wait_send)
-    pl.when(has_right)(from_left.wait_send)
-
 
 def local(gx_size, gy_size, populations, fluid):
     padded = (NX + 2, NY + 2 * TOP, NZ)
     vmem, dma = pltpu.VMEM, pltpu.SemaphoreType.DMA
     f32 = jnp.float32
-    velocity, magnitude = pl.pallas_call(
+    blurred = pl.pallas_call(
         functools.partial(kernel, gx_size, gy_size),
-        out_shape=(
-            jax.ShapeDtypeStruct((3, 2, 2, 128), f32),
-            jax.ShapeDtypeStruct((2, 2, 128), f32),
-        ),
+        out_shape=jax.ShapeDtypeStruct((16, 128), f32),
         in_specs=[pl.BlockSpec(memory_space=pltpu.HBM)] * 2,
-        out_specs=(pl.BlockSpec(memory_space=pltpu.VMEM),) * 2,
+        out_specs=pl.BlockSpec(memory_space=pltpu.VMEM),
         scratch_shapes=[
             vmem((19, NX, NY, NZ), f32),
-            vmem((19, *padded), f32),
-            vmem((19, *padded), f32),
-            vmem((3, *padded), jnp.int32),
+            vmem((NX, NY, NZ), jnp.int32),
+            vmem((len(ORDER), *padded), f32),
+            vmem((len(ORDER), *padded), f32),
+            vmem((3, *padded), f32),
             vmem((256, 128), f32),
             vmem((32, 128), f32),
             vmem((128, 256), f32),
             vmem((16, 128), f32),
             vmem((3, 16, 128), f32),
             vmem((16, 128), f32),
-            vmem((16, 128), f32),
             pltpu.SemaphoreType.REGULAR((4,)),
             dma((8,)),
             dma,
-            dma((8,)),
-            dma((8,)),
             dma((2, 9)),
             dma((2, 9)),
             dma((3,)),
@@ -482,6 +504,16 @@
             collective_id=0, has_side_effects=True, vmem_limit_bytes=55200 * 1024
         ),
     )(populations, fluid)
+    velocity, magnitude = pl.pallas_call(
+        finish,
+        out_shape=(
+            jax.ShapeDtypeStruct((3, 2, 2, 128), f32),
+            jax.ShapeDtypeStruct((2, 2, 128), f32),
+        ),
+        in_specs=[pl.BlockSpec(memory_space=pltpu.VMEM)],
+        out_specs=(pl.BlockSpec(memory_space=pltpu.VMEM),) * 2,
+        compiler_params=pltpu.CompilerParams(vmem_limit_bytes=1024 * 1024),
+    )(blurred)
     return jnp.swapaxes(velocity, 2, 3), jnp.swapaxes(magnitude, 1, 2)
 
 

time: 27.9 us -> 26.7 us (0.957)
  local copies, waits for them, and re-layouts: 1.17 us -> 0 us
    unnamed x2 -> x0, local copies, waits for them, and re-layouts: 1.17 us -> none
    pallas_call x1 -> x2, Pallas kernels: 25.9 us -> 26 us  [the longest x1 25.4 us: local(): pl.pallas_call(functools.partial(kernel, gx_size, gy_size), out_shape=jax...]
where the time goes in v4:
time: 26.7 us; the launch traced here: 26.6 us
  Pallas kernels  26 us (97%)
  between operations  0.64 us (2%)
    pallas_call x1, Pallas kernels, local(): pl.pallas_call(functools.partial(kernel, gx_size, gy_size), out_shape=jax...  25.4 us
    pallas_call x1, Pallas kernels, local(): pl.pallas_call(finish, out_shape=(jax.ShapeDtypeStruct((3, 2, 2, 128), f3...  0.61 us

profile of v4, /device:TPU:7, one launch (start us, length us, event | category | flops | bytes accessed | tf_op | source)
XLA Modules:
  0.0 26.6 jit_solution(12320761205969682204)
XLA Ops:
  0.6 25.4 %shard_map.41.final = f32[16,128]{1,0:T(8,128)S(1)} custom-call(f32[19,8,32,128]{3,2,1,0:T(8,128)} %populations.1, s32[8,32,128]{2,1,0:T(8,128)} %fluid.1), custom_call_target="tpu_custom_call" | custom-call | tf_op jit(solution)/shard_map/pallas_call | solution.py:478
  26.0 0.6 %shard_map.42 = (f32[3,2,2,128]{3,2,1,0:T(2,128)}, f32[2,2,128]{2,1,0:T(2,128)}) custom-call(f32[16,128]{1,0:T(8,128)S(1)} %shard_map.41.final), custom_call_target="tpu_custom_call" | custom-call | tf_op jit(solution)/shard_map/pallas_call | solution.py:507

commit v5 on v4

--- a/solution.py
+++ b/solution.py
@@ -129,6 +129,22 @@
     has_left, has_right = gx > 0, gx < gx_size - 1
     has_below, has_above = gy > 0, gy < gy_size - 1
 
+    def number(*conditions):
+        return sum(condition.astype(jnp.int32) for condition in conditions)
+
+    barrier = pltpu.get_barrier_semaphore()
+    beside_x = ((-1, has_left), (1, has_right), (0, None))
+    beside_y = ((-1, has_below), (0, None), (1, has_above))
+    for dx, in_x in beside_x:
+        for dy, in_y in beside_y:
+            if dx == 0 and dy == 0:
+                continue
+            there = in_y if in_x is None else in_x if in_y is None else in_x & in_y
+
+            @pl.when(there)
+            def _():
+                pl.semaphore_signal(barrier, inc=1, device_id=(gx + dx, gy + dy), device_id_type=MESH)
+
     def load(x):
         return pltpu.make_async_copy(populations.at[:, x], start.at[:, x], load_sem.at[x])
 
@@ -138,22 +154,6 @@
     fluid_copy.start()
     for x in range(1, NX - 1):
         load(x).start()
-
-    def number(*conditions):
-        return sum(condition.astype(jnp.int32) for condition in conditions)
-
-    barrier = pltpu.get_barrier_semaphore()
-    beside_x = ((-1, has_left), (0, None), (1, has_right))
-    beside_y = ((-1, has_below), (0, None), (1, has_above))
-    for dx, in_x in beside_x:
-        for dy, in_y in beside_y:
-            if dx == 0 and dy == 0:
-                continue
-            there = in_y if in_x is None else in_x if in_y is None else in_x & in_y
-
-            @pl.when(there)
-            def _():
-                pl.semaphore_signal(barrier, inc=1, device_id=(gx + dx, gy + dy), device_id_type=MESH)
 
     def tell(stage):
         for way in (-(2**stage), 2**stage):
@@ -286,12 +286,16 @@
     distance = jnp.abs(2 * (row & 15) + (row >> 4) - (lane >> 2))
     zmat[...] = jnp.where(distance == 0, 0.5, jnp.where(distance == 1, 0.25, 0.0)).astype(jnp.float32)
 
+    turn = 8 * gy + 8
+
     def y_rows(step, carry):
         at = pl.multiple_of(8 * step, 8)
-        row = lax.broadcasted_iota(jnp.int32, (8, 256), 0) + at
+        row = (lax.broadcasted_iota(jnp.int32, (8, 256), 0) + (at - turn + 256)) & 127
         column = lax.broadcasted_iota(jnp.int32, (8, 256), 1)
-        hit = (((row >> 3) & 7) == 7 - (column >> 5)) & ((row & 7) == ((column >> 2) & 7))
-        ymat[pl.ds(at, 8), :] = jnp.where(hit, 1.0, 0.0).astype(jnp.float32)
+        hit = (((row >> 4) & 3) == 3 - (column >> 6)) & ((row & 7) == ((column >> 2) & 7))
+        same = ((row >> 3) & 1) != ((column >> 5) & 1)
+        ymat[pl.ds(at, 8), :] = jnp.where(hit, jnp.where(same, 0.5, 0.25), 0.0)
+        ymat[pl.ds(pl.multiple_of(at + 128, 8), 8), :] = jnp.where(hit & ~same, 0.25, 0.0)
         return carry
 
     lax.fori_loop(0, 16, y_rows, 0)
@@ -335,12 +339,12 @@
     for x in range(1, NX - 1):
         load(x).wait()
     over_slabs(relax_tile, False, outer)
-    over_slabs(relax_tile, False, middle)
     pl.semaphore_wait(barrier, (1 + number(has_left, has_right)) * (1 + number(has_below, has_above)) - 1)
     first_x.start()
     first_y.start()
     tell(0)
 
+    over_slabs(relax_tile, False, middle)
     lax.fori_loop(0, NX, inner_walls, 0)
     over_slabs(step_tile, False, middle)
     hear(0)
@@ -387,13 +391,15 @@
         for part in parts(over_y)
     )
     lane = lax.broadcasted_iota(jnp.int32, (16, 128), 1)
-    table[...] = jnp.where(lane >= 64, over_z[:16], over_z[16:])
-
+    first_z = ((lane - turn + 256) & 64) != 0
+    for part in range(2):
+        lanes = slice(128 * part, 128 * part + 128)
+        table[part] = jnp.where(first_z, over_z[:16, lanes], over_z[16:, lanes])
     hear(3)
 
     def exchange(place, x, partner):
         return pltpu.make_async_remote_copy(
-            src_ref=table.at[pl.ds(partner, 1)],
+            src_ref=table.at[min(place, 1), pl.ds(partner, 1)],
             dst_ref=gathered.at[place, pl.ds(gy, 1)],
             send_sem=all_send.at[place],
             recv_sem=all_recv.at[place],
@@ -401,23 +407,21 @@
             device_id_type=MESH,
         )
 
-    def send(place, x, begin, end):
-        for step in range(begin, end):
+    def send(place, x, steps):
+        for step in steps:
             exchange(place, x, lax.rem(gy + step, gy_size)).start()
 
-    far = (gy_size // 2 - 3, gy_size // 2 + 4)
-    send(0, gx, *far)
-    pl.when(has_left)(lambda: send(2, gx - 1, *far))
-    pl.when(has_right)(lambda: send(1, gx + 1, *far))
-    send(0, gx, far[1], gy_size)
-    send(0, gx, 1, far[0])
-    pl.when(has_left)(lambda: send(2, gx - 1, far[1], gy_size + far[0]))
-    pl.when(has_right)(lambda: send(1, gx + 1, far[1], gy_size + far[0]))
-    gathered[0, pl.ds(gy, 1), :] = table[pl.ds(gy, 1), :]
+    middle_step = gy_size // 2
+    steps = sorted(range(gy_size), key=lambda step: abs(step - middle_step))
+    for some in (steps[:7], steps[7:]):
+        pl.when(has_left)(lambda: send(2, gx - 1, some))
+        pl.when(has_right)(lambda: send(1, gx + 1, some))
+        send(0, gx, [step for step in some if step])
+    gathered[0, pl.ds(gy, 1), :] = table[0, pl.ds(gy, 1), :]
 
     def everyone(place, count):
         return pltpu.make_async_remote_copy(
-            src_ref=table.at[pl.ds(0, count)],
+            src_ref=table.at[min(place, 1), pl.ds(0, count)],
             dst_ref=gathered.at[place, pl.ds(0, count)],
             send_sem=all_send.at[place],
             recv_sem=all_recv.at[place],
@@ -435,17 +439,10 @@
     pl.when(has_left)(from_left.wait_recv)
     pl.when(has_right)(from_right.wait_recv)
 
-    lower = (lane & 8) != 0
-    own = gathered[0]
-    beside = jnp.where(
-        lower,
-        pltpu.roll(own, 8, 1) + pltpu.roll(gathered[1], 8, 1),
-        pltpu.roll(own, 120, 1) + pltpu.roll(gathered[2], 120, 1),
-    )
-    along_x = pltpu.roll(0.5 * own + 0.25 * beside, 8, 1)
-
-    mixed[pl.ds(0, 8), :] = pltpu.roll(along_x[:8], 0, 1, stride=8, stride_axis=0)
-    mixed[pl.ds(8, 8), :] = pltpu.roll(along_x[8:], 64, 1, stride=8, stride_axis=0)
+    row = lax.broadcasted_iota(jnp.int32, (16, 128), 0)
+    lower = (((lane >> 3) - row) & 1) == 0
+    mixed[...] = gathered[0] + jnp.where(lower, gathered[1], gathered[2])
+
     lane = lax.broadcasted_iota(jnp.int32, (8, 128), 1)
     halves = [jnp.zeros((8, 128), jnp.float32) for _ in range(2)]
     for source in range(gy_size):
@@ -488,8 +485,8 @@
             vmem((3, *padded), f32),
             vmem((256, 128), f32),
             vmem((32, 128), f32),
-            vmem((128, 256), f32),
-            vmem((16, 128), f32),
+            vmem((256, 256), f32),
+            vmem((2, 16, 128), f32),
             vmem((3, 16, 128), f32),
             vmem((16, 128), f32),
             pltpu.SemaphoreType.REGULAR((4,)),

time: 26.7 us -> 26.3 us (0.985)
  Pallas kernels: 26 us -> 25.5 us
    pallas_call x1, Pallas kernels: 25.4 us -> 24.9 us  [local(): pl.pallas_call(functools.partial(kernel, gx_size, gy_size), out_shape=jax...]
where the time goes in v5:
time: 26.3 us; the launch traced here: 26.2 us
  Pallas kernels  25.5 us (97%)
  between operations  0.64 us (2%)
    pallas_call x1, Pallas kernels, local(): pl.pallas_call(functools.partial(kernel, gx_size, gy_size), out_shape=jax...  24.9 us
    pallas_call x1, Pallas kernels, local(): pl.pallas_call(finish, out_shape=(jax.ShapeDtypeStruct((3, 2, 2, 128), f3...  0.61 us

profile of v5, /device:TPU:7, one launch (start us, length us, event | category | flops | bytes accessed | tf_op | source)
XLA Modules:
  0.0 26.2 jit_solution(11605852631165629939)
XLA Ops:
  0.6 24.9 %shard_map.41.final = f32[16,128]{1,0:T(8,128)S(1)} custom-call(f32[19,8,32,128]{3,2,1,0:T(8,128)} %populations.1, s32[8,32,128]{2,1,0:T(8,128)} %fluid.1), custom_call_target="tpu_custom_call" | custom-call | tf_op jit(solution)/shard_map/pallas_call | solution.py:475
  25.5 0.6 %shard_map.42 = (f32[3,2,2,128]{3,2,1,0:T(2,128)}, f32[2,2,128]{2,1,0:T(2,128)}) custom-call(f32[16,128]{1,0:T(8,128)S(1)} %shard_map.41.final), custom_call_target="tpu_custom_call" | custom-call | tf_op jit(solution)/shard_map/pallas_call | solution.py:504

commit v6 on v5

--- a/solution.py
+++ b/solution.py
@@ -192,15 +192,23 @@
     low, high = pl.ds(TOP - 1, 1), pl.ds(LAST + 1, 1)
     bottom, top = pl.ds(TOP, 1), pl.ds(LAST, 1)
 
-    def x_sides(flags):
-        return [
+    def x_sides(flags, cut):
+        sides = []
+        for start_row, count in ((TOP, cut), (TOP + cut, NY - cut)):
+            rows = pl.ds(start_row, count)
+            sides += [
+                (pl.ds(1, 5 + flags), (NX, rows), (0, rows), (1, 0), has_right, has_left),
+                (pl.ds(11, 5 + flags), (1, rows), (NX + 1, rows), (-1, 0), has_left, has_right),
+            ]
+        below_corners = [
+            (pl.ds(1 - flags, 1 + flags), (NX, bottom), (0, high), (1, -1), has_right & has_below, has_left & has_above),
+            (pl.ds(15, 1 + flags), (1, bottom), (NX + 1, high), (-1, -1), has_left & has_below, has_right & has_above),
+        ]
+        above_corners = [
             (pl.ds(5, 1 + flags), (NX, top), (0, low), (1, 1), has_right & has_above, has_left & has_below),
-            (pl.ds(1 - flags, 1 + flags), (NX, bottom), (0, high), (1, -1), has_right & has_below, has_left & has_above),
             (pl.ds(11 - flags, 1 + flags), (1, top), (NX + 1, low), (-1, 1), has_left & has_above, has_right & has_below),
-            (pl.ds(15, 1 + flags), (1, bottom), (NX + 1, high), (-1, -1), has_left & has_below, has_right & has_above),
-            (pl.ds(1, 5 + flags), (NX, block), (0, block), (1, 0), has_right, has_left),
-            (pl.ds(11, 5 + flags), (1, block), (NX + 1, block), (-1, 0), has_left, has_right),
         ]
+        return below_corners + sides[:2] + above_corners + sides[2:]
 
     y_sides = [
         (pl.ds(5, 7), (inner, top), (inner, low), (0, 1), has_above, has_below),
@@ -226,22 +234,24 @@
                 for i, (channels, source, target, way, sent, arrives) in enumerate(sides)
             ]
 
-        def start(self):
-            for copy, sent, _ in self.copies:
+        def start(self, *which):
+            for i in which or range(len(self.copies)):
+                copy, sent, _ = self.copies[i]
                 pl.when(sent)(copy.start)
 
-        def wait_recv(self):
-            for copy, _, arrives in self.copies:
+        def wait_recv(self, *which):
+            for i in which or range(len(self.copies)):
+                copy, _, arrives = self.copies[i]
                 pl.when(arrives)(copy.wait_recv)
 
         def wait_send(self):
             for copy, sent, _ in self.copies:
                 pl.when(sent)(copy.wait_send)
 
-    first_x = Sides(first, x_sides(1), halo_send.at[0], halo_recv.at[0], 0)
-    first_y = Sides(first, y_sides, halo_send.at[0], halo_recv.at[0], 6)
-    second_x = Sides(second, x_sides(0), halo_send.at[1], halo_recv.at[1], 0)
-    second_y = Sides(second, y_sides, halo_send.at[1], halo_recv.at[1], 6)
+    first_x = Sides(first, x_sides(1, 17), halo_send.at[0], halo_recv.at[0], 0)
+    first_y = Sides(first, y_sides, halo_send.at[0], halo_recv.at[0], 8)
+    second_x = Sides(second, x_sides(0, 16), halo_send.at[1], halo_recv.at[1], 0)
+    second_y = Sides(second, y_sides, halo_send.at[1], halo_recv.at[1], 8)
 
     def relax_tile(x, tile):
         rows = pl.ds(8 * tile, 8)
@@ -263,18 +273,15 @@
             sums[rows, :] = sums[rows, :] + value
 
     def over_slabs(body, edge, tiles):
-        def edge_slab(step, carry):
-            for tile in tiles:
-                body((NX - 1) * (1 - step), tile)
-            return carry
-
         def inner_slab(x, carry):
             for tile in tiles:
                 body(x, tile)
             return carry
 
         if edge:
-            lax.fori_loop(0, 2, edge_slab, 0)
+            for tile in tiles:
+                for x in (NX - 1, 0):
+                    body(x, tile)
         else:
             lax.fori_loop(1, NX - 1, inner_slab, 0)
 
@@ -340,7 +347,7 @@
         load(x).wait()
     over_slabs(relax_tile, False, outer)
     pl.semaphore_wait(barrier, (1 + number(has_left, has_right)) * (1 + number(has_below, has_above)) - 1)
-    first_x.start()
+    first_x.start(0, 1, 4, 5, 2, 3, 6, 7)
     first_y.start()
     tell(0)
 
@@ -357,16 +364,26 @@
     over_slabs(step_tile, False, outer)
     hear(1)
     tell(2)
-    first_x.wait_recv()
-    for slot, slab in ((6, 0), (16, NX + 1)):
-        for tile in range(TILES):
-            rows = pl.ds(TOP + 8 * tile, 8)
-            walls[0, slab, rows, :] = first[slot, slab, rows, :]
-            lane_walls(slab, rows)
-    for slot, slab, row in ((6, 0, low), (0, 0, high), (10, NX + 1, low), (16, NX + 1, high)):
+    first_x.wait_recv(2, 3, 4, 5)
+    for slot, slab, row in ((6, 0, low), (10, NX + 1, low), (6, 0, pl.ds(TOP + 16, 1)), (16, NX + 1, pl.ds(TOP + 16, 1))):
         walls[0, slab, row, :] = first[slot, slab, row, :]
-    over_slabs(step_tile, True, every)
-    second_x.start()
+
+    def halo_walls(tiles):
+        for slot, slab in ((6, 0), (16, NX + 1)):
+            for tile in tiles:
+                rows = pl.ds(TOP + 8 * tile, 8)
+                walls[0, slab, rows, :] = first[slot, slab, rows, :]
+                lane_walls(slab, rows)
+
+    halo_walls((0, 1))
+    over_slabs(step_tile, True, (0, 1))
+    second_x.start(0, 1, 2, 3)
+    first_x.wait_recv(0, 1, 6, 7)
+    for slot, slab, row in ((0, 0, high), (16, NX + 1, high)):
+        walls[0, slab, row, :] = first[slot, slab, row, :]
+    halo_walls((2, 3))
+    over_slabs(step_tile, True, (2, 3))
+    second_x.start(4, 5, 6, 7)
     second_y.start()
     hear(2)
     tell(3)
@@ -492,8 +509,8 @@
             pltpu.SemaphoreType.REGULAR((4,)),
             dma((8,)),
             dma,
-            dma((2, 9)),
-            dma((2, 9)),
+            dma((2, 11)),
+            dma((2, 11)),
             dma((3,)),
             dma((3,)),
         ],

time: 26.3 us -> 25.9 us (0.985)
  Pallas kernels: 25.5 us -> 25.1 us
    pallas_call x1, Pallas kernels: 24.9 us -> 24.5 us  [local(): pl.pallas_call(functools.partial(kernel, gx_size, gy_size), out_shape=jax...]
where the time goes in v6:
time: 25.9 us; the launch traced here: 25.8 us
  Pallas kernels  25.1 us (97%)
  between operations  0.64 us (2%)
    pallas_call x1, Pallas kernels, local(): pl.pallas_call(functools.partial(kernel, gx_size, gy_size), out_shape=jax...  24.5 us
    pallas_call x1, Pallas kernels, local(): pl.pallas_call(finish, out_shape=(jax.ShapeDtypeStruct((3, 2, 2, 128), f3...  0.61 us

profile of v6, /device:TPU:7, one launch (start us, length us, event | category | flops | bytes accessed | tf_op | source)
XLA Modules:
  0.0 25.8 jit_solution(9846086525162147110)
XLA Ops:
  0.6 24.5 %shard_map.41.final = f32[16,128]{1,0:T(8,128)S(1)} custom-call(f32[19,8,32,128]{3,2,1,0:T(8,128)} %populations.1, s32[8,32,128]{2,1,0:T(8,128)} %fluid.1), custom_call_target="tpu_custom_call" | custom-call | tf_op jit(solution)/shard_map/pallas_call | solution.py:492
  25.2 0.6 %shard_map.42 = (f32[3,2,2,128]{3,2,1,0:T(2,128)}, f32[2,2,128]{2,1,0:T(2,128)}) custom-call(f32[16,128]{1,0:T(8,128)S(1)} %shard_map.41.final), custom_call_target="tpu_custom_call" | custom-call | tf_op jit(solution)/shard_map/pallas_call | solution.py:521

commit v7 on v6

--- a/solution.py
+++ b/solution.py
@@ -291,21 +291,21 @@
     row = lax.broadcasted_iota(jnp.int32, (32, NZ), 0)
     lane = lax.broadcasted_iota(jnp.int32, (32, NZ), 1)
     distance = jnp.abs(2 * (row & 15) + (row >> 4) - (lane >> 2))
-    zmat[...] = jnp.where(distance == 0, 0.5, jnp.where(distance == 1, 0.25, 0.0)).astype(jnp.float32)
+    zmat[...] = jnp.where(distance == 0, 0.5, jnp.where(distance == 1, 0.25, 0.0)).astype(jnp.bfloat16)
 
     turn = 8 * gy + 8
 
     def y_rows(step, carry):
-        at = pl.multiple_of(8 * step, 8)
-        row = (lax.broadcasted_iota(jnp.int32, (8, 256), 0) + (at - turn + 256)) & 127
-        column = lax.broadcasted_iota(jnp.int32, (8, 256), 1)
+        at = pl.multiple_of(16 * step, 16)
+        row = (lax.broadcasted_iota(jnp.int32, (16, 256), 0) + (at - turn + 256)) & 127
+        column = lax.broadcasted_iota(jnp.int32, (16, 256), 1)
         hit = (((row >> 4) & 3) == 3 - (column >> 6)) & ((row & 7) == ((column >> 2) & 7))
         same = ((row >> 3) & 1) != ((column >> 5) & 1)
-        ymat[pl.ds(at, 8), :] = jnp.where(hit, jnp.where(same, 0.5, 0.25), 0.0)
-        ymat[pl.ds(pl.multiple_of(at + 128, 8), 8), :] = jnp.where(hit & ~same, 0.25, 0.0)
+        ymat[pl.ds(at, 16), :] = jnp.where(hit, jnp.where(same, 0.5, 0.25), 0.0).astype(jnp.bfloat16)
+        ymat[pl.ds(pl.multiple_of(at + 128, 16), 16), :] = jnp.where(hit & ~same, 0.25, 0.0).astype(jnp.bfloat16)
         return carry
 
-    lax.fori_loop(0, 16, y_rows, 0)
+    lax.fori_loop(0, 8, y_rows, 0)
 
     @pl.when(gx == 0)
     def _():
@@ -400,9 +400,9 @@
         upper = value.astype(jnp.bfloat16)
         return upper, (value - upper.astype(jnp.float32)).astype(jnp.bfloat16)
 
-    weights = ymat[...].astype(jnp.bfloat16)
+    weights = ymat[...]
     over_y = sum(jnp.dot(weights, part, preferred_element_type=jnp.float32) for part in parts(sums[...]))
-    weights = zmat[...].astype(jnp.bfloat16)
+    weights = zmat[...]
     over_z = sum(
         lax.dot_general(weights, part, (((1,), (1,)), ((), ())), preferred_element_type=jnp.float32)
         for part in parts(over_y)
@@ -431,9 +431,9 @@
     middle_step = gy_size // 2
     steps = sorted(range(gy_size), key=lambda step: abs(step - middle_step))
     for some in (steps[:7], steps[7:]):
-        pl.when(has_left)(lambda: send(2, gx - 1, some))
         pl.when(has_right)(lambda: send(1, gx + 1, some))
         send(0, gx, [step for step in some if step])
+        pl.when(has_left)(lambda: send(2, gx - 1, some))
     gathered[0, pl.ds(gy, 1), :] = table[0, pl.ds(gy, 1), :]
 
     def everyone(place, count):
@@ -478,10 +478,10 @@
     for x in range(2):
         for z in range(2):
             fraction = final[pl.ds(8 * z + 6 + x, 1), :]
-            divisor = jnp.maximum(fraction, 1.0)
+            scale = 1.0 / (jnp.maximum(fraction, 1.0) * velocity_scale)
             for component in range(3):
                 voxels = final[pl.ds(8 * z + 2 * component + x, 1), :]
-                velocity_ref[component, x, pl.ds(z, 1), :] = voxels / divisor / velocity_scale
+                velocity_ref[component, x, pl.ds(z, 1), :] = voxels * scale
             magnitude_ref[x, pl.ds(z, 1), :] = fraction / 64.0
 
 
@@ -501,8 +501,8 @@
             vmem((len(ORDER), *padded), f32),
             vmem((3, *padded), f32),
             vmem((256, 128), f32),
-            vmem((32, 128), f32),
-            vmem((256, 256), f32),
+            vmem((32, 128), jnp.bfloat16),
+            vmem((256, 256), jnp.bfloat16),
             vmem((2, 16, 128), f32),
             vmem((3, 16, 128), f32),
             vmem((16, 128), f32),

time: 25.9 us -> 25.8 us (level)
  no operation moved by 1% of the time
where the time goes in v7:
time: 25.8 us; the launch traced here: 25.7 us
  Pallas kernels  25.1 us (97%)
  between operations  0.64 us (2%)
    pallas_call x1, Pallas kernels, local(): pl.pallas_call(functools.partial(kernel, gx_size, gy_size), out_shape=jax...  24.5 us
    pallas_call x1, Pallas kernels, local(): pl.pallas_call(finish, out_shape=(jax.ShapeDtypeStruct((3, 2, 2, 128), f3...  0.61 us

profile of v7, /device:TPU:7, one launch (start us, length us, event | category | flops | bytes accessed | tf_op | source)
XLA Modules:
  0.0 25.7 jit_solution(18292942513405836505)
XLA Ops:
  0.6 24.5 %shard_map.41.final = f32[16,128]{1,0:T(8,128)S(1)} custom-call(f32[19,8,32,128]{3,2,1,0:T(8,128)} %populations.1, s32[8,32,128]{2,1,0:T(8,128)} %fluid.1), custom_call_target="tpu_custom_call" | custom-call | tf_op jit(solution)/shard_map/pallas_call | solution.py:492
  25.1 0.6 %shard_map.42 = (f32[3,2,2,128]{3,2,1,0:T(2,128)}, f32[2,2,128]{2,1,0:T(2,128)}) custom-call(f32[16,128]{1,0:T(8,128)S(1)} %shard_map.41.final), custom_call_target="tpu_custom_call" | custom-call | tf_op jit(solution)/shard_map/pallas_call | solution.py:521

commit v8 on v7

--- a/solution.py
+++ b/solution.py
@@ -401,7 +401,11 @@
         return upper, (value - upper.astype(jnp.float32)).astype(jnp.bfloat16)
 
     weights = ymat[...]
-    over_y = sum(jnp.dot(weights, part, preferred_element_type=jnp.float32) for part in parts(sums[...]))
+    over_y = jnp.dot(
+        jnp.concatenate([weights, weights], axis=1),
+        jnp.concatenate(parts(sums[...]), axis=0),
+        preferred_element_type=jnp.float32,
+    )
     weights = zmat[...]
     over_z = sum(
         lax.dot_general(weights, part, (((1,), (1,)), ((), ())), preferred_element_type=jnp.float32)

time: 25.8 us -> 25.8 us (level)
  no operation moved by 1% of the time
where the time goes in v8:
time: 25.8 us; the launch traced here: 25.7 us
  Pallas kernels  25.1 us (97%)
  between operations  0.64 us (2%)
    pallas_call x1, Pallas kernels, local(): pl.pallas_call(functools.partial(kernel, gx_size, gy_size), out_shape=jax...  24.5 us
    pallas_call x1, Pallas kernels, local(): pl.pallas_call(finish, out_shape=(jax.ShapeDtypeStruct((3, 2, 2, 128), f3...  0.61 us

profile of v8, /device:TPU:7, one launch (start us, length us, event | category | flops | bytes accessed | tf_op | source)
XLA Modules:
  0.0 25.7 jit_solution(14555851196553903362)
XLA Ops:
  0.6 24.5 %shard_map.41.final = f32[16,128]{1,0:T(8,128)S(1)} custom-call(f32[19,8,32,128]{3,2,1,0:T(8,128)} %populations.1, s32[8,32,128]{2,1,0:T(8,128)} %fluid.1), custom_call_target="tpu_custom_call" | custom-call | tf_op jit(solution)/shard_map/pallas_call | solution.py:496
  25.1 0.6 %shard_map.42 = (f32[3,2,2,128]{3,2,1,0:T(2,128)}, f32[2,2,128]{2,1,0:T(2,128)}) custom-call(f32[16,128]{1,0:T(8,128)S(1)} %shard_map.41.final), custom_call_target="tpu_custom_call" | custom-call | tf_op jit(solution)/shard_map/pallas_call | solution.py:525

commit v9 on v8

--- a/solution.py
+++ b/solution.py
@@ -434,7 +434,7 @@
 
     middle_step = gy_size // 2
     steps = sorted(range(gy_size), key=lambda step: abs(step - middle_step))
-    for some in (steps[:7], steps[7:]):
+    for some in (steps[:3], steps[3:7], steps[7:]):
         pl.when(has_right)(lambda: send(1, gx + 1, some))
         send(0, gx, [step for step in some if step])
         pl.when(has_left)(lambda: send(2, gx - 1, some))

time: 25.8 us -> 25.8 us (level)
  no operation moved by 1% of the time
where the time goes in v9:
time: 25.8 us; the launch traced here: 25.7 us
  Pallas kernels  25.1 us (97%)
  between operations  0.64 us (2%)
    pallas_call x1, Pallas kernels, local(): pl.pallas_call(functools.partial(kernel, gx_size, gy_size), out_shape=jax...  24.5 us
    pallas_call x1, Pallas kernels, local(): pl.pallas_call(finish, out_shape=(jax.ShapeDtypeStruct((3, 2, 2, 128), f3...  0.61 us

profile of v9, /device:TPU:7, one launch (start us, length us, event | category | flops | bytes accessed | tf_op | source)
XLA Modules:
  0.0 25.7 jit_solution(16153084194407240000)
XLA Ops:
  0.6 24.5 %shard_map.41.final = f32[16,128]{1,0:T(8,128)S(1)} custom-call(f32[19,8,32,128]{3,2,1,0:T(8,128)} %populations.1, s32[8,32,128]{2,1,0:T(8,128)} %fluid.1), custom_call_target="tpu_custom_call" | custom-call | tf_op jit(solution)/shard_map/pallas_call | solution.py:496
  25.1 0.6 %shard_map.42 = (f32[3,2,2,128]{3,2,1,0:T(2,128)}, f32[2,2,128]{2,1,0:T(2,128)}) custom-call(f32[16,128]{1,0:T(8,128)S(1)} %shard_map.41.final), custom_call_target="tpu_custom_call" | custom-call | tf_op jit(solution)/shard_map/pallas_call | solution.py:525
